TPU v7x, 32 devices: a whole 2x2x4 slice. The times are simulated.
32 devices in a mesh: groups: 2 (over y), tile: 4 (over z), scan: 4 (over x, core).
Axes of the slice: x: 2, y: 2, z: 4, core: 2. Of those that a mesh axis runs over, the one named last changes fastest.
Arguments:
- object_field: float32 [2, 3072, 384], P(None, ('groups', 'tile')), parts along dimension 1, may hold values from -5 to 5
- probe_field: float32 [2, 512, 256], P(None, 'groups'), parts along dimension 1, may hold values from -6 to 6
- amplitudes: bfloat16 [8, 4, 4, 256, 256], P(('groups', 'tile'), 'scan'), parts along dimension 0, may hold values from 0.099609375 to 3
- anchors: int32 [8, 4, 4, 2], P(('groups', 'tile'), 'scan'), parts along dimension 0, may hold values from 8 to 376, as said below
- jitter: int32 [8, 4, 4, 2], P(('groups', 'tile'), 'scan'), parts along dimension 0, may hold values from -8 to 8
- counts: int32 [8, 4], P(('groups', 'tile'), 'scan'), parts along dimension 0, may hold values from 1 to 4, as said below
Outputs:
- object_out: float32 [2, 3072, 384], P(None, ('groups', 'tile')), parts along dimension 1
- probe_out: float32 [2, 512, 256], P(None, 'groups'), parts along dimension 1
There are 2 independent parts, one for each index of `groups`. A program takes and returns all parts, laid end to end along the dimension named above; each array names one. Nothing has to cross between parts.
Inputs may be any that keep to these rules, and one draw needn't show every extreme that they name: `anchors`: with the jitter, a slot's row start lies in 0 to 384 within its tile, and its 256 rows stay within the tile and the next one; in the last tile they stay within the tile. Columns keep the window within the object. `counts`: slots at or after a device's count are not live; some device is full in every draw.
All inputs are finite; a program needn't handle non-finite values.
Results may differ from a plain program's by a relative error of at most 0.0063.
Values sent between devices are 32-bit elements; how exact they have to be, the bound alone decides.
A program may use at most 64 MiB of HBM per device.

v0:
```python
import math

import jax
import jax.numpy as jnp
from jax import lax
from jax.sharding import PartitionSpec as P

ITERS = 2


object_rate = 0.25


def from_behind(shard, axis, by):
    count = lax.axis_size(axis)
    pairs = [(i, i + by) for i in range(count) if 0 <= i + by < count]
    return lax.ppermute(shard, axis, pairs)


def tables(wave_size):
    indices = jnp.arange(wave_size, dtype=jnp.int32)
    angles = (indices[:, None] * indices[None, :] % wave_size).astype(jnp.float32) * (
        2.0 * math.pi / wave_size
    )
    cosine = jnp.cos(angles) / math.sqrt(wave_size)
    sines = jnp.sin(angles) / math.sqrt(wave_size)
    table_a = jnp.concatenate(
        [jnp.concatenate([cosine, sines], 1), jnp.concatenate([-sines, cosine], 1)], 0
    )
    table_b = jnp.concatenate(
        [jnp.concatenate([cosine, -sines], 1), jnp.concatenate([sines, cosine], 1)], 0
    )
    return (table_a.astype(jnp.bfloat16), table_b.astype(jnp.bfloat16))


def transform(waves, left_table, right_table):
    number, _, wave_size, _ = waves.shape
    stacked = waves.reshape(number, 2 * wave_size, wave_size)
    sectioned = jnp.einsum("ij,bjk->bik", left_table, stacked, preferred_element_type=jnp.float32)
    sectioned = sectioned.astype(jnp.bfloat16).reshape(number, 2, wave_size, wave_size)
    sectioned = sectioned.transpose(0, 2, 1, 3).reshape(number, wave_size, 2 * wave_size)
    result = jnp.einsum("bij,jk->bik", sectioned, right_table, preferred_element_type=jnp.float32)
    return result.reshape(number, wave_size, 2, wave_size).transpose(0, 2, 1, 3)


def scan_terms(patches, probe_field, measured, active, table_a, table_b):
    probe_re, probe_im = (probe_field[0], probe_field[1])
    patch_re, patch_im = (patches[:, 0], patches[:, 1])
    exit_wave = jnp.stack(
        [probe_re * patch_re - probe_im * patch_im, probe_re * patch_im + probe_im * patch_re], 1
    ).astype(jnp.bfloat16)
    spectrum = transform(exit_wave, table_a, table_b)
    power = spectrum[:, 0] ** 2 + spectrum[:, 1] ** 2
    factor = (measured.astype(jnp.float32) / jnp.sqrt(power + 0.25) - 1.0) * active[:, None, None]
    residual = (spectrum * factor[:, None]).astype(jnp.bfloat16)
    near_field = transform(residual, table_b, table_a)
    near_re, near_im = (near_field[:, 0], near_field[:, 1])
    object_step = jnp.stack(
        [probe_re * near_re + probe_im * near_im, probe_re * near_im - probe_im * near_re], 1
    )
    probe_step = jnp.stack(
        [
            jnp.sum(patch_re * near_re + patch_im * near_im, 0),
            jnp.sum(patch_re * near_im - patch_im * near_re, 0),
        ],
        0,
    )
    return (object_step, probe_step)


def body(object_field, probe_field, amplitudes, anchors, jitter, counts):
    rows_here = object_field.shape[1]
    wave_size = probe_field.shape[1]
    slot_count = amplitudes.shape[2]
    table_a, table_b = tables(wave_size)
    root = jnp.zeros((), jnp.int32)
    starts = (anchors + jitter)[0, 0]
    row_start = starts[:, 0]
    col_start = starts[:, 1]
    active = (jnp.arange(slot_count, dtype=jnp.int32) < counts[0, 0]).astype(jnp.float32)
    measured = amplitudes[0, 0]
    total_scans = slot_count * lax.axis_size("tile") * lax.axis_size("scan")
    for iteration in range(ITERS):
        lower_rim = from_behind(object_field, "tile", -1)[:, :wave_size, :]
        padded = jnp.concatenate([object_field, lower_rim], 1)

        def window(row_one, col_one):
            return lax.dynamic_slice(padded, (root, row_one, col_one), (2, wave_size, wave_size))

        patches = jax.vmap(window)(row_start, col_start)
        object_step, probe_step = scan_terms(
            patches, probe_field, measured, active, table_a, table_b
        )

        def add_slot(slot, accum):
            current = lax.dynamic_slice(
                accum, (root, row_start[slot], col_start[slot]), (2, wave_size, wave_size)
            )
            return lax.dynamic_update_slice(
                accum, current + object_step[slot], (root, row_start[slot], col_start[slot])
            )

        gradient = lax.fori_loop(0, slot_count, add_slot, jnp.zeros(padded.shape, jnp.float32))
        returned = from_behind(gradient[:, rows_here:, :], "tile", 1)
        owned = gradient[:, :rows_here, :].at[:, :wave_size, :].add(returned)
        strength = jnp.max(probe_field[0] ** 2 + probe_field[1] ** 2) + 1e-06
        summed = lax.psum(owned, "scan")
        object_field = object_field + object_rate * summed / strength
        probe_field = probe_field + lax.psum(probe_step, ("tile", "scan")) / math.sqrt(total_scans)
    return (object_field, probe_field)


def solution(mesh):
    in_specs = (
        P(None, ("groups", "tile"), None),
        P(None, "groups", None),
        P(("groups", "tile"), "scan", None, None, None),
        P(("groups", "tile"), "scan", None, None),
        P(("groups", "tile"), "scan", None, None),
        P(("groups", "tile"), "scan"),
    )
    out_specs = (P(None, ("groups", "tile"), None), P(None, "groups", None))
    return jax.shard_map(body, mesh=mesh, in_specs=in_specs, out_specs=out_specs, check_vma=False)
```

profile of v0, /device:TPU:0, one launch (start us, length us, event | category | flops | bytes accessed | tf_op | source)
XLA Modules:
  0.0 569.5 jit_solution(5218843685718358646)
XLA Ops:
  8.0 1.3 collective-permute-start
  16.2 23.0 %collective-permute-done = f32[2,384,384]{2,1,0:T(8,128)} collective-permute-done((f32[2,384,384]{2,1,0:T(8,128)}, f32[2,384,384]{2,1,0:T(8,128)}, u32[]{:S(2)}, u32[]{:S(2)}) %collective-permute-start) | collective-permute-done | bytes 1179680 | tf_op jit(solution)/shard_map/ppermute | solution.py:17
  40.5 1.4 pad_maximum_fusion.2
  42.0 12.9 %while.32 = (s32[]{:T(128)}, f32[2,640,384]{2,1,0:T(8,128)}, s32[4,3]{1,0:T(4,128)S(1)}, f32[4,2,256,256]{3,2,1,0:T(8,128)S(1)}, s32[]{:T(128)}) while((s32[]{:T(128)}, f32[2,640,384]{2,1,0:T(8,128)}, s32[4,3]{1,0:T(4,128)S(1)}, f32[4,2,256,256]{3,2,1,0:T(8,128)S(1)}, s32[]{:T(128)}) %tuple.110), condition=%wide.while_cond.2, body=%wide.while_body.2.sunk | while | flops 2 | bytes 1048693 | solution.py:88
  42.7 2.5 bitcast_dynamic-update-slice_fusion.4
  45.9 2.5 bitcast_dynamic-update-slice_fusion.4
  49.2 2.5 bitcast_dynamic-update-slice_fusion.4
  52.4 2.5 bitcast_dynamic-update-slice_fusion.4
  57.1 1.7 fusion
  58.9 2.2 reshape.138
  61.0 5.8 %copy.10 = bf16[4,256,2,256]{3,2,1,0:T(2,128)(2,1)} copy(bf16[4,256,2,256]{1,2,3,0:T(2,128)(2,1)} %bitcast.154) | data formatting | bytes 2097152 | tf_op jit(solution)/shard_map/transpose | solution.py:41
  66.8 2.5 reshape.196
  69.3 2.0 convolution_bitcast_fusion.3
  72.7 1.7 fusion.1
  74.4 2.2 reshape.141
  76.6 5.8 %copy.13 = bf16[4,256,2,256]{3,2,1,0:T(2,128)(2,1)} copy(bf16[4,256,2,256]{1,2,3,0:T(2,128)(2,1)} %bitcast.155) | data formatting | bytes 2097152 | tf_op jit(solution)/shard_map/transpose | solution.py:41
  82.4 2.5 reshape.199
  84.9 2.0 convolution_bitcast_fusion.2
  86.9 1.4 add_reduce_fusion.1
  88.3 1.5 pad_maximum_fusion
  89.9 59.0 %while.30 = (s32[]{:T(128)}, f32[2,640,384]{2,1,0:T(8,128)S(1)}, s32[4]{0:T(128)S(1)}, s32[4]{0:T(128)S(1)}, f32[4,2,256,256]{3,2,1,0:T(8,128)}, /*index=5*/s32[]{:T(128)}, s32[]{:T(128)}, s32[]{:T(128)}, s32[]{:T(128)}) while((s32[]{:T(128)}, f32[2,640,384]{2,1,0:T(8,128)S(1)}, s32[4]{0:T(128)S(1)}, s32[4]{0:T(128)S(1)}, ...), condition=%wide.region_1.2_spmd, body=%wide.region_0.1_spmd.sunk | while | flops 131080 | bytes 2621641 | solution.py:103
  94.9 1.3 bitcast_add_fusion.4
  96.2 7.0 %dynamic_update_slice.16 = f32[2,640,384]{2,1,0:T(8,128)S(1)} dynamic-update-slice(f32[2,640,384]{2,1,0:T(8,128)S(1)} %get-tuple-element.453, f32[2,256,256]{2,1,0:T(8,128)S(1)} %bitcast_add_fusion.4, s32[]{:T(128)} %constant.147.clone.1..sunk, s32[]{:T(128)S(6)} %select_n.101, s32[]{:T(128)S(6)} %select_n.102) | dynamic-update-slice | bytes 1048580 | tf_op jit(solution)/shard_map/while/body/eval_jaxpr/dynamic_update_slice | solution.py:99
  109.5 9.4 %dynamic_update_slice.16 = f32[2,640,384]{2,1,0:T(8,128)S(1)} dynamic-update-slice(f32[2,640,384]{2,1,0:T(8,128)S(1)} %get-tuple-element.453, f32[2,256,256]{2,1,0:T(8,128)S(1)} %bitcast_add_fusion.4, s32[]{:T(128)} %constant.147.clone.1..sunk, s32[]{:T(128)S(6)} %select_n.101, s32[]{:T(128)S(6)} %select_n.102) | dynamic-update-slice | bytes 1048580 | tf_op jit(solution)/shard_map/while/body/eval_jaxpr/dynamic_update_slice | solution.py:99
  124.0 1.3 bitcast_add_fusion.4
  125.3 9.2 %dynamic_update_slice.16 = f32[2,640,384]{2,1,0:T(8,128)S(1)} dynamic-update-slice(f32[2,640,384]{2,1,0:T(8,128)S(1)} %get-tuple-element.453, f32[2,256,256]{2,1,0:T(8,128)S(1)} %bitcast_add_fusion.4, s32[]{:T(128)} %constant.147.clone.1..sunk, s32[]{:T(128)S(6)} %select_n.101, s32[]{:T(128)S(6)} %select_n.102) | dynamic-update-slice | bytes 1048580 | tf_op jit(solution)/shard_map/while/body/eval_jaxpr/dynamic_update_slice | solution.py:99
  140.8 8.0 %dynamic_update_slice.16 = f32[2,640,384]{2,1,0:T(8,128)S(1)} dynamic-update-slice(f32[2,640,384]{2,1,0:T(8,128)S(1)} %get-tuple-element.453, f32[2,256,256]{2,1,0:T(8,128)S(1)} %bitcast_add_fusion.4, s32[]{:T(128)} %constant.147.clone.1..sunk, s32[]{:T(128)S(6)} %select_n.101, s32[]{:T(128)S(6)} %select_n.102) | dynamic-update-slice | bytes 1048580 | tf_op jit(solution)/shard_map/while/body/eval_jaxpr/dynamic_update_slice | solution.py:99
  148.9 5.5 collective-permute-start.1
  155.5 13.3 %collective-permute-done.1 = f32[2,256,384]{2,1,0:T(8,128)S(1)} collective-permute-done((f32[2,256,384]{2,1,0:T(8,128)S(1)}, f32[2,256,384]{2,1,0:T(8,128)S(1)}, u32[]{:S(2)}, u32[]{:S(2)}) %collective-permute-start.1) | collective-permute-done | bytes 786464 | tf_op jit(solution)/shard_map/ppermute | solution.py:17
  171.3 39.8 %all-reduce.5.cloned.1.call-done = f32[2,384,384]{2,1,0:T(8,128)} async-done(((f32[2,384,384]{2,1,0:T(8,128)}), f32[2,384,384]{2,1,0:T(8,128)}) %all-reduce.5.cloned.1.call-update) | async-done | bytes 1179664 | tf_op jit(solution)/shard_map/psum | solution.py:107
  211.1 1.7 divide_add_fusion.1
  212.9 1.3 collective-permute-start.2
  215.3 92.8 %all-reduce.7.cloned.1.call-done = f32[2,256,256]{2,1,0:T(8,128)} async-done(((f32[2,256,256]{2,1,0:T(8,128)}), f32[2,256,256]{2,1,0:T(8,128)}) %all-reduce.7.cloned.1.call-update) | async-done | bytes 524304 | tf_op jit(solution)/shard_map/psum | solution.py:109
  311.1 1.4 pad_maximum_fusion.3
  312.7 13.2 %while.33 = (s32[]{:T(128)}, f32[2,640,384]{2,1,0:T(8,128)}, s32[4,3]{1,0:T(4,128)S(1)}, f32[4,2,256,256]{3,2,1,0:T(8,128)S(1)}, s32[]{:T(128)}) while((s32[]{:T(128)}, f32[2,640,384]{2,1,0:T(8,128)}, s32[4,3]{1,0:T(4,128)S(1)}, f32[4,2,256,256]{3,2,1,0:T(8,128)S(1)}, s32[]{:T(128)}) %tuple.130), condition=%wide.while_cond.3, body=%wide.while_body.3.sunk | while | flops 2 | bytes 1048693 | solution.py:88
  313.4 2.6 bitcast_dynamic-update-slice_fusion.5
  316.7 2.6 bitcast_dynamic-update-slice_fusion.5
  320.0 2.6 bitcast_dynamic-update-slice_fusion.5
  323.3 2.6 bitcast_dynamic-update-slice_fusion.5
  328.2 1.7 fusion.2
  329.9 2.2 reshape.143
  332.1 5.8 %copy.17 = bf16[4,256,2,256]{3,2,1,0:T(2,128)(2,1)} copy(bf16[4,256,2,256]{1,2,3,0:T(2,128)(2,1)} %bitcast.156) | data formatting | bytes 2097152 | tf_op jit(solution)/shard_map/transpose | solution.py:41
  337.9 2.5 reshape.201
  340.4 2.2 convolution_bitcast_fusion.1
  343.9 1.7 fusion.3
  345.6 2.2 reshape.146
  347.8 5.8 %copy.20 = bf16[4,256,2,256]{3,2,1,0:T(2,128)(2,1)} copy(bf16[4,256,2,256]{1,2,3,0:T(2,128)(2,1)} %bitcast.157) | data formatting | bytes 2097152 | tf_op jit(solution)/shard_map/transpose | solution.py:41
  353.5 2.5 reshape.203
  356.1 2.0 convolution_bitcast_fusion
  358.7 1.5 pad_maximum_fusion.1
  360.3 59.0 %while.31 = (s32[]{:T(128)}, f32[2,640,384]{2,1,0:T(8,128)S(1)}, s32[4]{0:T(128)S(1)}, s32[4]{0:T(128)S(1)}, f32[4,2,256,256]{3,2,1,0:T(8,128)}, /*index=5*/s32[]{:T(128)}, s32[]{:T(128)}, s32[]{:T(128)}, s32[]{:T(128)}) while((s32[]{:T(128)}, f32[2,640,384]{2,1,0:T(8,128)S(1)}, s32[4]{0:T(128)S(1)}, s32[4]{0:T(128)S(1)}, ...), condition=%wide.region_8.9_spmd, body=%wide.region_7.8_spmd.sunk | while | flops 131080 | bytes 2621641 | solution.py:103
  365.3 1.3 bitcast_add_fusion.5
  366.6 7.0 %dynamic_update_slice.17 = f32[2,640,384]{2,1,0:T(8,128)S(1)} dynamic-update-slice(f32[2,640,384]{2,1,0:T(8,128)S(1)} %get-tuple-element.495, f32[2,256,256]{2,1,0:T(8,128)S(1)} %bitcast_add_fusion.5, s32[]{:T(128)} %constant.147.clone.1..sunk.1, s32[]{:T(128)S(6)} %select_n.103, s32[]{:T(128)S(6)} %select_n.104) | dynamic-update-slice | bytes 1048580 | tf_op jit(solution)/shard_map/while/body/eval_jaxpr/dynamic_update_slice | solution.py:99
  379.9 9.4 %dynamic_update_slice.17 = f32[2,640,384]{2,1,0:T(8,128)S(1)} dynamic-update-slice(f32[2,640,384]{2,1,0:T(8,128)S(1)} %get-tuple-element.495, f32[2,256,256]{2,1,0:T(8,128)S(1)} %bitcast_add_fusion.5, s32[]{:T(128)} %constant.147.clone.1..sunk.1, s32[]{:T(128)S(6)} %select_n.103, s32[]{:T(128)S(6)} %select_n.104) | dynamic-update-slice | bytes 1048580 | tf_op jit(solution)/shard_map/while/body/eval_jaxpr/dynamic_update_slice | solution.py:99
  394.4 1.3 bitcast_add_fusion.5
  395.7 9.2 %dynamic_update_slice.17 = f32[2,640,384]{2,1,0:T(8,128)S(1)} dynamic-update-slice(f32[2,640,384]{2,1,0:T(8,128)S(1)} %get-tuple-element.495, f32[2,256,256]{2,1,0:T(8,128)S(1)} %bitcast_add_fusion.5, s32[]{:T(128)} %constant.147.clone.1..sunk.1, s32[]{:T(128)S(6)} %select_n.103, s32[]{:T(128)S(6)} %select_n.104) | dynamic-update-slice | bytes 1048580 | tf_op jit(solution)/shard_map/while/body/eval_jaxpr/dynamic_update_slice | solution.py:99
  411.2 8.0 %dynamic_update_slice.17 = f32[2,640,384]{2,1,0:T(8,128)S(1)} dynamic-update-slice(f32[2,640,384]{2,1,0:T(8,128)S(1)} %get-tuple-element.495, f32[2,256,256]{2,1,0:T(8,128)S(1)} %bitcast_add_fusion.5, s32[]{:T(128)} %constant.147.clone.1..sunk.1, s32[]{:T(128)S(6)} %select_n.103, s32[]{:T(128)S(6)} %select_n.104) | dynamic-update-slice | bytes 1048580 | tf_op jit(solution)/shard_map/while/body/eval_jaxpr/dynamic_update_slice | solution.py:99
  420.2 7.6 %collective-permute-start.3 = (f32[2,256,384]{2,1,0:T(8,128)}, f32[2,256,384]{2,1,0:T(8,128)}, u32[]{:S(2)}, u32[]{:S(2)}) collective-permute-start(f32[2,256,384]{2,1,0:T(8,128)} %slice.151), channel_id=1, source_target_pairs={{0,4},{4,8},{8,12},{1,5},{5,9},{9,13},{2,6},{6,10},{10,14},{3,7},{... | collective-permute-start | bytes 2359304 | tf_op jit(solution)/shard_map/ppermute | solution.py:17
  429.8 11.8 %collective-permute-done.3 = f32[2,256,384]{2,1,0:T(8,128)} collective-permute-done((f32[2,256,384]{2,1,0:T(8,128)}, f32[2,256,384]{2,1,0:T(8,128)}, u32[]{:S(2)}, u32[]{:S(2)}) %collective-permute-start.3) | collective-permute-done | bytes 786464 | tf_op jit(solution)/shard_map/ppermute | solution.py:17
  441.6 2.1 add_dynamic-update-slice_fusion
  445.1 74.4 %all-reduce.11.cloned.1.call-done = f32[2,256,256]{2,1,0:T(8,128)} async-done(((f32[2,256,256]{2,1,0:T(8,128)}), f32[2,256,256]{2,1,0:T(8,128)}) %all-reduce.11.cloned.1.call-update) | async-done | bytes 524304 | tf_op jit(solution)/shard_map/psum | solution.py:109
  519.5 1.9 multiply_add_fusion.2
  521.4 38.1 %all-reduce.9.cloned.1.call-done = f32[2,384,384]{2,1,0:T(8,128)} async-done(((f32[2,384,384]{2,1,0:T(8,128)}), f32[2,384,384]{2,1,0:T(8,128)}) %all-reduce.9.cloned.1.call-update) | async-done | bytes 1179664 | tf_op jit(solution)/shard_map/psum | solution.py:107
  559.5 2.4 divide_add_fusion
  (131 shorter events, 45.8 us)
Async XLA Ops:
  8.0 203.1 %all-reduce.5.cloned.1.call-start = ((), (), s32[]{:S(2)}) async-start(), calls=%async_computation | async-start | bytes 2359296 | tf_op jit(solution)/shard_map/psum | solution.py:107
  8.0 31.2 %collective-permute-start = (f32[2,384,384]{2,1,0:T(8,128)}, f32[2,384,384]{2,1,0:T(8,128)}, u32[]{:S(2)}, u32[]{:S(2)}) collective-permute-start(f32[2,384,384]{2,1,0:T(8,128)} %param.14), channel_id=1, source_target_pairs={{4,0},{8,4},{12,8},{5,1},{9,5},{13,9},{6,2},{10,6},{14,10},{7,3},{... | collective-permute-start | bytes 3538952 | tf_op jit(solution)/shard_map/ppermute | solution.py:17
  10.2 5.3 copy-start.3
  11.2 60.9 %copy-start.12 = (bf16[256,256]{1,0:T(8,128)(2,1)}, bf16[256,256]{1,0:T(8,128)(2,1)S(1)}, u32[]{:S(2)}) copy-start(bf16[256,256]{1,0:T(8,128)(2,1)S(1)} %fusion.32) | copy-start | bytes 393220
  12.3 0.9 copy-start.14
  12.3 0.9 copy-start.19
  13.4 55.9 %copy-start.2 = (bf16[512,512]{1,0:T(8,128)(2,1)}, bf16[512,512]{1,0:T(8,128)(2,1)S(1)}, u32[]{:S(2)}) copy-start(bf16[512,512]{1,0:T(8,128)(2,1)S(1)} %copy.30) | copy-start | bytes 1572868
  13.4 27.0 %copy-start.5 = (f32[2,384,384]{2,1,0:T(8,128)S(1)}, f32[2,384,384]{2,1,0:T(8,128)}, u32[]{:S(2)}) copy-start(f32[2,384,384]{2,1,0:T(8,128)} %param.14) | copy-start | bytes 3538948
  56.2 0.9 copy-start.15
  56.2 1.0 copy-start.20
  69.3 2.0 copy-start.8
  71.7 0.9 copy-start.16
  71.7 1.0 copy-start.21
  84.9 2.0 copy-start.7
  148.9 19.9 %collective-permute-start.1 = (f32[2,256,384]{2,1,0:T(8,128)S(1)}, f32[2,256,384]{2,1,0:T(8,128)S(1)}, u32[]{:S(2)}, u32[]{:S(2)}) collective-permute-start(f32[2,256,384]{2,1,0:T(8,128)S(1)} %slice.139), channel_id=1, source_target_pairs={{0,4},{4,8},{8,12},{1,5},{5,9},{9,13},{2,6},{6,10},{10,14},{3,7},{... | collective-permute-start | bytes 2359304 | tf_op jit(solution)/shard_map/ppermute | solution.py:17
  155.5 14.4 %copy-start.4 = (f32[2,256,256]{2,1,0:T(8,128)S(1)}, f32[2,256,256]{2,1,0:T(8,128)}, u32[]{:S(2)}) copy-start(f32[2,256,256]{2,1,0:T(8,128)} %param.15) | copy-start | bytes 1572868
  169.8 44.3 %copy-start.10 = (f32[256,256]{1,0:T(8,128)S(1)}, f32[256,256]{1,0:T(8,128)}, u32[]{:S(2)}) copy-start(f32[256,256]{1,0:T(8,128)} %get-tuple-element.242) | copy-start | bytes 786436
  169.8 44.3 %copy-start.11 = (f32[256,256]{1,0:T(8,128)S(1)}, f32[256,256]{1,0:T(8,128)}, u32[]{:S(2)}) copy-start(f32[256,256]{1,0:T(8,128)} %get-tuple-element.243) | copy-start | bytes 786436
  169.9 138.2 %all-reduce.7.cloned.1.call-start = ((), (), s32[]{:S(2)}) async-start(), calls=%async_computation.1 | async-start | bytes 1048576 | tf_op jit(solution)/shard_map/psum | solution.py:109
  212.8 98.3 %copy-start = (f32[2,384,384]{2,1,0:T(8,128)}, f32[2,384,384]{2,1,0:T(8,128)S(1)}, u32[]{:S(2)}) copy-start(f32[2,384,384]{2,1,0:T(8,128)S(1)} %divide_add_fusion.1) | copy-start | bytes 3538948
  212.9 97.1 %collective-permute-start.2 = (f32[2,384,384]{2,1,0:T(8,128)S(1)}, f32[2,384,384]{2,1,0:T(8,128)}, u32[]{:S(2)}, u32[]{:S(2)}) collective-permute-start(f32[2,384,384]{2,1,0:T(8,128)S(1)} %divide_add_fusion.1), channel_id=1, source_target_pairs={{4,0},{8,4},{12,8},{5,1},{9,5},{13,9},{6,2},{10,6},{14,10},{7,3},{... | collective-permute-start | bytes 3538952 | tf_op jit(solution)/shard_map/ppermute | solution.py:17
  215.0 304.5 %all-reduce.11.cloned.1.call-start = ((), (), s32[]{:S(2)}) async-start(), calls=%async_computation.3 | async-start | bytes 1048576 | tf_op jit(solution)/shard_map/psum | solution.py:109
  327.2 0.9 copy-start.13
  327.2 1.0 copy-start.17
  327.2 1.0 copy-start.22
  340.4 2.2 copy-start.9
  342.9 0.9 copy-start.18
  342.9 1.0 copy-start.23
  356.1 2.0 copy-start.6
  420.2 21.4 %collective-permute-start.3 = (f32[2,256,384]{2,1,0:T(8,128)}, f32[2,256,384]{2,1,0:T(8,128)}, u32[]{:S(2)}, u32[]{:S(2)}) collective-permute-start(f32[2,256,384]{2,1,0:T(8,128)} %slice.151), channel_id=1, source_target_pairs={{0,4},{4,8},{8,12},{1,5},{5,9},{9,13},{2,6},{6,10},{10,14},{3,7},{... | collective-permute-start | bytes 2359304 | tf_op jit(solution)/shard_map/ppermute | solution.py:17
  429.7 129.8 %all-reduce.9.cloned.1.call-start = ((), (), s32[]{:S(2)}) async-start(), calls=%async_computation.2 | async-start | bytes 2359296 | tf_op jit(solution)/shard_map/psum | solution.py:107
  443.7 115.8 %copy-start.1 = (f32[2,384,384]{2,1,0:T(8,128)S(1)}, f32[2,384,384]{2,1,0:T(8,128)}, u32[]{:S(2)}) copy-start(f32[2,384,384]{2,1,0:T(8,128)} %copy-done) | copy-start | bytes 3538948
Sparse Core Ops, SparseCore 0:
  170.0 41.0 all-reduce.4
Sparse Core Ops, SparseCore 1:
  215.1 92.9 all-reduce.6
  429.8 89.6 all-reduce.10
  521.8 37.7 all-reduce.8
where the time goes:
time: 572 us; the launch traced here: 570 us
  waiting for transfers between devices  293 us (51%)
  local copies, waits for them, and re-layouts  157 us (27%)
  other arithmetic  38.8 us (7%)
  loops' own time  31.5 us (6%)
  between operations  18.2 us (3%)
  starting transfers between devices  16 us (3%)
  matrix products  15.1 us (3%)
    psum x2, waiting for transfers between devices, body(): lax.psum(probe_step, ('tile', 'scan')) / math.sqrt(total_scans)  167 us
    psum x2, waiting for transfers between devices, body(): summed = lax.psum(owned, 'scan')  77.9 us
    dynamic_update_slice x8, local copies, waits for them, and re-layouts, add_slot(): lax.dynamic_update_slice(accum, current + object_step[slot], (root, row_s...  67.1 us
    ppermute x4, waiting for transfers between devices, from_behind(): return lax.ppermute(shard, axis, pairs)  48.2 us
    another operation x2, loops' own time, body(): lax.fori_loop(0, slot_count, add_slot, jnp.zeros(padded.shape, jnp.float32))  31.3 us
    gather x24, local copies, waits for them, and re-layouts  25.9 us
    transpose x4, local copies, waits for them, and re-layouts, transform(): sectioned.transpose(0, 2, 1, 3).reshape(number, wave_size, 2 * wave_size)  23.1 us
    ppermute x4, starting transfers between devices, from_behind(): return lax.ppermute(shard, axis, pairs)  15.7 us
  transfers between devices with their start and end apart: 8, of which 7 were waited for; matrix products, arithmetic and copies ran while one was open for 3% of the time, Pallas kernels for 0%

commit v1 on v0

v1 whole, which is shorter than its diff:
```python
import functools
import math

import jax
import jax.numpy as jnp
import numpy as np
from jax import lax
from jax.experimental import pallas as pl
from jax.experimental.pallas import tpu as pltpu
from jax.sharding import PartitionSpec as P

ITERS = 2
RATE = 0.25
CORES = 2
LANES = 128
CHUNK = 32


def tables(wave):
    index = np.arange(wave)
    angles = (index[:, None] * index[None, :] % wave) * (2.0 * math.pi / wave)
    cosine = np.cos(angles) / math.sqrt(wave)
    sines = np.sin(angles) / math.sqrt(wave)
    table_a = np.block([[cosine, sines], [-sines, cosine]])
    table_b = np.block([[cosine, -sines], [sines, cosine]])
    return (jnp.asarray(table_a, jnp.bfloat16), jnp.asarray(table_b, jnp.bfloat16))


def scan_kernel(
    starts, counts, padded, probe, amps, table_a, table_b, grad, probe_grad,
    window, terms, patch, waves, sections, field,
):
    slots, wave, _ = amps.shape
    columns = padded.shape[2]
    pieces = columns // LANES
    wide = wave // LANES
    lane = lax.broadcasted_iota(jnp.int32, (CHUNK, LANES), 1)

    for part in range(2):
        for p in range(pieces):
            window[part, p] = padded[part, :, p * LANES : (p + 1) * LANES]
    terms[...] = jnp.zeros(terms.shape, jnp.float32)
    probe_grad[...] = jnp.zeros(probe_grad.shape, jnp.float32)

    def dot(left, right):
        return jnp.dot(left, right, preferred_element_type=jnp.float32)

    def slot_step(slot, carry):
        row = starts[slot, 0]
        col = starts[slot, 1]
        live = jnp.where(slot < counts[0], 1.0, 0.0).astype(jnp.float32)
        back = lax.rem(LANES - lax.rem(col, LANES), LANES)
        ahead = lax.rem(col, LANES)
        skip = lax.div(col, LANES)
        low = lane < LANES - ahead
        high = lane >= ahead

        for top in range(0, wave, CHUNK):
            halves = []
            for part in range(2):
                turned = [
                    pltpu.roll(
                        window[part, p, pl.ds(row + top, CHUNK), :], back, 1
                    )
                    for p in range(pieces)
                ]
                turned.append(turned[-1])
                lanes_out = []
                for w in range(wide):
                    best = None
                    for k in range(pieces - wide + 1):
                        this = jnp.where(low, turned[w + k], turned[w + k + 1])
                        best = this if best is None else jnp.where(skip == k, this, best)
                    lanes_out.append(best)
                halves.append(jnp.concatenate(lanes_out, 1))
            real, imag = halves
            patch[0, top : top + CHUNK, :] = real
            patch[1, top : top + CHUNK, :] = imag
            p_re = probe[0, top : top + CHUNK, :]
            p_im = probe[1, top : top + CHUNK, :]
            waves[top : top + CHUNK, :] = (p_re * real - p_im * imag).astype(jnp.bfloat16)
            waves[wave + top : wave + top + CHUNK, :] = (p_re * imag + p_im * real).astype(
                jnp.bfloat16
            )

        sectioned = dot(table_a[...], waves[...]).astype(jnp.bfloat16)
        sections[:, :wave] = sectioned[:wave]
        sections[:, wave:] = sectioned[wave:]
        field[...] = dot(sections[...], table_b[...])

        for top in range(0, wave, CHUNK):
            real = field[top : top + CHUNK, :wave]
            imag = field[top : top + CHUNK, wave:]
            power = real * real + imag * imag
            measured = amps[slot, top : top + CHUNK, :].astype(jnp.float32)
            factor = (measured * lax.rsqrt(power + 0.25) - 1.0) * live
            waves[top : top + CHUNK, :] = (real * factor).astype(jnp.bfloat16)
            waves[wave + top : wave + top + CHUNK, :] = (imag * factor).astype(jnp.bfloat16)

        sectioned = dot(table_b[...], waves[...]).astype(jnp.bfloat16)
        sections[:, :wave] = sectioned[:wave]
        sections[:, wave:] = sectioned[wave:]
        field[...] = dot(sections[...], table_a[...])

        for top in range(0, wave, CHUNK):
            real = field[top : top + CHUNK, :wave]
            imag = field[top : top + CHUNK, wave:]
            p_re = probe[0, top : top + CHUNK, :]
            p_im = probe[1, top : top + CHUNK, :]
            w_re = patch[0, top : top + CHUNK, :]
            w_im = patch[1, top : top + CHUNK, :]
            probe_grad[0, top : top + CHUNK, :] += w_re * real + w_im * imag
            probe_grad[1, top : top + CHUNK, :] += w_re * imag - w_im * real
            steps = (p_re * real + p_im * imag, p_re * imag - p_im * real)
            for part in range(2):
                turned = [
                    pltpu.roll(steps[part][:, w * LANES : (w + 1) * LANES], ahead, 1)
                    for w in range(wide)
                ]
                zero = jnp.zeros((CHUNK, LANES), jnp.float32)

                def block(index):
                    return turned[index] if 0 <= index < wide else zero

                for p in range(pieces):
                    best = None
                    for k in range(pieces - wide + 1):
                        this = jnp.where(high, block(p - k), block(p - k - 1))
                        best = this if best is None else jnp.where(skip == k, this, best)
                    terms[part, p, pl.ds(row + top, CHUNK), :] += best
        return carry

    lax.fori_loop(0, slots, slot_step, 0)
    for part in range(2):
        for p in range(pieces):
            grad[part, :, p * LANES : (p + 1) * LANES] = terms[part, p]


def scan_terms(starts, counts, padded, probe, amps, table_a, table_b):
    slots, wave, _ = amps.shape
    _, extent, columns = padded.shape
    blocks = pltpu.VMEM((2, columns // LANES, extent, LANES), jnp.float32)
    vmem = pl.BlockSpec(memory_space=pltpu.VMEM)
    smem = pl.BlockSpec(memory_space=pltpu.SMEM)
    return pl.pallas_call(
        scan_kernel,
        out_shape=(
            jax.ShapeDtypeStruct(padded.shape, jnp.float32),
            jax.ShapeDtypeStruct(probe.shape, jnp.float32),
        ),
        in_specs=[smem, smem, vmem, vmem, vmem, vmem, vmem],
        out_specs=(vmem, vmem),
        scratch_shapes=[
            blocks,
            blocks,
            pltpu.VMEM((2, wave, wave), jnp.float32),
            pltpu.VMEM((2 * wave, wave), jnp.bfloat16),
            pltpu.VMEM((wave, 2 * wave), jnp.bfloat16),
            pltpu.VMEM((wave, 2 * wave), jnp.float32),
        ],
        compiler_params=pltpu.CompilerParams(vmem_limit_bytes=32 * 1024 * 1024),
        name="scan_terms",
    )(starts, counts, padded, probe, amps, table_a, table_b)


class Links:
    def __init__(self, send, recv, n_tile, n_scan):
        self.send, self.recv = send, recv
        self.used = 0
        self.drain = []
        self.n_tile = n_tile
        self.chips = n_scan // CORES
        self.tile = lax.axis_index("tile")
        self.scan = lax.axis_index("scan")
        self.chip = self.scan // CORES
        self.core = self.scan % CORES

    def other_core(self):
        return {"scan": self.chip * CORES + 1 - self.core}

    def chip_at(self, step):
        return (self.chip + step) % self.chips

    def on_chip(self, step):
        return {"scan": self.chip_at(step) * CORES + self.core}

    def greet(self, tiles):
        barrier = pltpu.get_barrier_semaphore()
        peers = [self.other_core()] + [self.on_chip(k) for k in range(1, self.chips)]
        peers += [{"tile": (self.tile + k) % self.n_tile} for k in tiles]
        for peer in peers:
            pl.semaphore_signal(
                barrier, inc=1, device_id=peer, device_id_type=pl.DeviceIdType.MESH
            )
        pl.semaphore_wait(barrier, len(peers))

    def copy(self, source, target, device, when=None):
        made = pltpu.make_async_remote_copy(
            src_ref=source,
            dst_ref=target,
            send_sem=self.send.at[self.used],
            recv_sem=self.recv.at[self.used],
            device_id=device,
            device_id_type=pl.DeviceIdType.MESH,
        )
        self.used += 1
        if when is None:
            made.start()
        else:
            pl.when(when)(made.start)
        self.drain.append((made, when))
        return made

    def finish(self):
        for made, when in self.drain:
            if when is None:
                made.wait_send()
            else:
                pl.when(when)(made.wait_send)


def on(when, action):
    if when is None:
        action()
    else:
        pl.when(when)(action)


def rim_kernel(n_tile, n_scan, wave, parts, own, padded, send, recv):
    links = Links(send, recv, n_tile, n_scan)
    rows = own.shape[1]
    chips, tile, core, chip = links.chips, links.tile, links.core, links.chip
    share = wave // chips
    some = share // parts
    above, below = tile > 0, tile < n_tile - 1
    tiles = sorted({1, n_tile - 1})
    links.greet(tiles)

    def at(owner, part, base):
        return pl.ds(base + owner * share + part * some, some)

    up = {"tile": (tile + n_tile - 1) % n_tile}
    first = [
        links.copy(own.at[core, at(chip, p, 0)], padded.at[core, at(chip, p, rows)], up, above)
        for p in range(parts)
    ]
    padded[:, :rows, :] = own[...]

    @pl.when(tile == n_tile - 1)
    def _():
        padded[:, rows:, :] = jnp.zeros((2, wave, own.shape[2]), jnp.float32)

    across, landed = [], []
    for p in range(parts):
        on(below, first[p].wait_recv)
        here = padded.at[core, at(chip, p, rows)]
        for k in range(1, chips):
            across.append((k, p, links.copy(here, here, links.on_chip(k), below)))
        landed.append(links.copy(here, here, links.other_core(), below))
    for k, p, made in across:
        on(below, made.wait_recv)
        here = padded.at[core, at(links.chip_at(chips - k), p, rows)]
        landed.append(links.copy(here, here, links.other_core(), below))
    for made in landed:
        on(below, made.wait_recv)
    links.finish()


def merge_kernel(
    n_tile, n_scan, scale, last, grad, probe_grad, old, probe, out, probe_out,
    core_in, core_probe, total, probe_total, rim_in, head_in, tail_in, probe_in,
    rim_sum, rim_back, probe_parts, send, recv,
):
    links = Links(send, recv, n_tile, n_scan)
    chips, tile, core, chip = links.chips, links.tile, links.core, links.chip
    wave = probe.shape[1]
    rows = grad.shape[1] - wave
    rest = rows - wave
    head, tail = wave // chips, rest // chips
    owners = probe_parts_of(n_tile, chips, wave)
    fine = head // owners
    above, below = tile > 0, tile < n_tile - 1
    down = {"tile": (tile + 1) % n_tile}
    up = {"tile": (tile + n_tile - 1) % n_tile}
    links.greet(range(1, n_tile))
    other = 1 - core
    partner = links.other_core()

    def to_core(first, count):
        span = pl.ds(first, count)
        return links.copy(grad.at[other, span], core_in.at[span], partner)

    got_rim = to_core(rows, wave)
    got_probe = links.copy(probe_grad.at[other], core_probe, partner)
    got_head = to_core(0, wave)
    got_tail = to_core(wave, rest)

    def fold(got, first, count, share, landing):
        got.wait_recv()
        span = pl.ds(first, count)
        total[span, :] = grad[core, span, :] + core_in[span, :]
        sent = []
        for k in range(1, chips):
            piece = total.at[pl.ds(first + links.chip_at(k) * share, share)]
            sent.append(links.copy(piece, landing.at[chip], links.on_chip(k)))
        return sent

    def gathered(sent, mine, landing):
        for made in sent:
            made.wait_recv()
        for k in range(1, chips):
            mine = mine + landing[links.chip_at(k)]
        return mine

    rim_sent = fold(got_rim, rows, wave, head, rim_in)
    got_probe.wait_recv()
    probe_total[...] = probe_grad[core] + core_probe[...]
    probe_sent = []
    for k in range(1, chips):
        piece = probe_total.at[pl.ds(links.chip_at(k) * head, head)]
        probe_sent.append(links.copy(piece, probe_in.at[chip], links.on_chip(k)))
    head_sent = fold(got_head, 0, wave, head, head_in)
    tail_sent = fold(got_tail, wave, rest, tail, tail_in)

    inverse = RATE / (
        jnp.max(probe[0] * probe[0] + probe[1] * probe[1], axis=(0, 1), keepdims=True) + 1e-06
    )

    rim_sum[...] = gathered(rim_sent, total[pl.ds(rows + chip * head, head), :], rim_in)
    rim_sent = links.copy(rim_sum, rim_back, down, below)

    mine = gathered(probe_sent, probe_total[pl.ds(chip * head, head), :], probe_in)
    probe_total[pl.ds(chip * head, head), :] = mine

    def owns(index):
        return None if owners == n_tile else index < owners

    spread = []
    for k in range(1, n_tile):
        to = (tile + k) % n_tile
        piece = jnp.minimum(to, owners - 1) if owners < n_tile else to
        spread.append(
            links.copy(
                probe_total.at[pl.ds(chip * head + piece * fine, fine)],
                probe_parts.at[tile],
                {"tile": to},
                owns(to),
            )
        )

    own_part = jnp.minimum(tile, owners - 1) if owners < n_tile else tile
    own_rows = pl.ds(chip * head + own_part * fine, fine)
    for made in spread:
        on(owns(tile), made.wait_recv)

    def close():
        sum_here = probe_total[own_rows, :]
        for k in range(1, n_tile):
            sum_here = sum_here + probe_parts[(tile + k) % n_tile]
        probe_out[core, own_rows, :] = probe[core, own_rows, :] + sum_here * scale

    on(owns(tile), close)
    place = probe_out.at[core, own_rows]
    probe_back = [
        links.copy(place, place, {"tile": (tile + k) % n_tile}, owns(tile))
        for k in range(1, n_tile)
    ]

    head_rows = pl.ds(chip * head, head)
    head_sum = gathered(head_sent, total[head_rows, :], head_in)
    on(above, rim_sent.wait_recv)
    back = jnp.where(above, rim_back[...], 0.0)
    out[core, head_rows, :] = old[core, head_rows, :] + inverse * (head_sum + back)
    here = out.at[core, head_rows]
    head_across = [links.copy(here, here, links.on_chip(k)) for k in range(1, chips)]
    rims = []
    if not last:
        rims.append(links.copy(here, out.at[core, pl.ds(rows + chip * head, head)], up, above))
    core_last = [(links.copy(here, here, partner), None)]

    tail_rows = pl.ds(wave + chip * tail, tail)
    tail_sum = gathered(tail_sent, total[tail_rows, :], tail_in)
    out[core, tail_rows, :] = old[core, tail_rows, :] + inverse * tail_sum
    here = out.at[core, tail_rows]
    tail_across = [links.copy(here, here, links.on_chip(k)) for k in range(1, chips)]
    core_last.append((links.copy(here, here, partner), None))

    for k, made in zip(range(1, n_tile), probe_back):
        on(owns((tile + n_tile - k) % n_tile), made.wait_recv)
    here = probe_out.at[core, pl.ds(chip * head, head)]
    probe_across = [links.copy(here, here, links.on_chip(k)) for k in range(1, chips)]
    core_last.append((links.copy(here, here, partner), None))

    for k in range(1, chips):
        head_across[k - 1].wait_recv()
        begin = links.chip_at(chips - k) * head
        here = out.at[core, pl.ds(begin, head)]
        if not last:
            rims.append(links.copy(here, out.at[core, pl.ds(rows + begin, head)], up, above))
        core_last.append((links.copy(here, here, partner), None))
    for k in range(1, chips):
        tail_across[k - 1].wait_recv()
        here = out.at[core, pl.ds(wave + links.chip_at(chips - k) * tail, tail)]
        core_last.append((links.copy(here, here, partner), None))
    for k in range(1, chips):
        probe_across[k - 1].wait_recv()
        here = probe_out.at[core, pl.ds(links.chip_at(chips - k) * head, head)]
        core_last.append((links.copy(here, here, partner), None))
    if not last:

        @pl.when(tile == n_tile - 1)
        def _():
            out[:, rows:, :] = jnp.zeros((2, wave, out.shape[2]), jnp.float32)

        for k, made in enumerate(rims):
            on(below, made.wait_recv)
            begin = links.chip_at((chips - k) % chips) * head
            here = out.at[core, pl.ds(rows + begin, head)]
            core_last.append((links.copy(here, here, partner, below), below))
    for made, when in core_last:
        on(when, made.wait_recv)
    links.finish()


def probe_parts_of(n_tile, chips, wave):
    owners = n_tile
    while (wave // chips) % owners or (wave // chips // owners) % 8:
        owners -= 1
    return owners


def first_rim(own, wave):
    n_tile, n_scan = lax.axis_size("tile"), lax.axis_size("scan")
    _, rows, columns = own.shape
    vmem = pl.BlockSpec(memory_space=pltpu.VMEM)
    parts = 2
    copies = parts * (2 * (n_scan // CORES) + 1)
    return pl.pallas_call(
        functools.partial(rim_kernel, n_tile, n_scan, wave, parts),
        out_shape=jax.ShapeDtypeStruct((2, rows + wave, columns), jnp.float32),
        in_specs=[vmem],
        out_specs=vmem,
        scratch_shapes=[pltpu.SemaphoreType.DMA((copies,)), pltpu.SemaphoreType.DMA((copies,))],
        compiler_params=pltpu.CompilerParams(
            collective_id=0, has_side_effects=True, vmem_limit_bytes=24 * 1024 * 1024
        ),
        name="first_rim",
    )(own)


def merge(grad, probe_grad, old, probe, scale, last, number):
    n_tile, n_scan = lax.axis_size("tile"), lax.axis_size("scan")
    chips = n_scan // CORES
    _, wave, _ = probe.shape
    _, extent, columns = grad.shape
    rows = extent - wave
    head, tail = wave // chips, (rows - wave) // chips
    fine = head // probe_parts_of(n_tile, chips, wave)
    vmem = pl.BlockSpec(memory_space=pltpu.VMEM)
    copies = 16 + 10 * chips + 2 * n_tile
    return pl.pallas_call(
        functools.partial(merge_kernel, n_tile, n_scan, scale, last),
        out_shape=(
            jax.ShapeDtypeStruct((2, rows if last else extent, columns), jnp.float32),
            jax.ShapeDtypeStruct(probe.shape, jnp.float32),
        ),
        in_specs=[vmem] * 4,
        out_specs=(vmem, vmem),
        scratch_shapes=[
            pltpu.VMEM((extent, columns), jnp.float32),
            pltpu.VMEM((wave, wave), jnp.float32),
            pltpu.VMEM((extent, columns), jnp.float32),
            pltpu.VMEM((wave, wave), jnp.float32),
            pltpu.VMEM((chips, head, columns), jnp.float32),
            pltpu.VMEM((chips, head, columns), jnp.float32),
            pltpu.VMEM((chips, tail, columns), jnp.float32),
            pltpu.VMEM((chips, head, wave), jnp.float32),
            pltpu.VMEM((head, columns), jnp.float32),
            pltpu.VMEM((head, columns), jnp.float32),
            pltpu.VMEM((n_tile, fine, wave), jnp.float32),
            pltpu.SemaphoreType.DMA((copies,)),
            pltpu.SemaphoreType.DMA((copies,)),
        ],
        compiler_params=pltpu.CompilerParams(
            collective_id=number, has_side_effects=True, vmem_limit_bytes=32 * 1024 * 1024
        ),
        name="merge_last" if last else "merge",
    )(grad, probe_grad, old, probe)


def body(object_field, probe_field, amplitudes, anchors, jitter, counts):
    wave = probe_field.shape[1]
    slots = amplitudes.shape[2]
    table_a, table_b = tables(wave)
    starts = (anchors + jitter)[0, 0]
    measured = amplitudes[0, 0]
    total_scans = slots * lax.axis_size("tile") * lax.axis_size("scan")
    scale = 1.0 / math.sqrt(total_scans)
    padded = first_rim(object_field, wave)
    probe = probe_field
    for iteration in range(ITERS):
        last = iteration == ITERS - 1
        grad, probe_grad = scan_terms(
            starts, counts[0], padded, probe, measured, table_a, table_b
        )
        padded, probe = merge(grad, probe_grad, padded, probe, scale, last, 1 + iteration)
    return (padded, probe)


def solution(mesh):
    in_specs = (
        P(None, ("groups", "tile"), None),
        P(None, "groups", None),
        P(("groups", "tile"), "scan", None, None, None),
        P(("groups", "tile"), "scan", None, None),
        P(("groups", "tile"), "scan", None, None),
        P(("groups", "tile"), "scan"),
    )
    out_specs = (P(None, ("groups", "tile"), None), P(None, "groups", None))
    return jax.shard_map(body, mesh=mesh, in_specs=in_specs, out_specs=out_specs, check_vma=False)
```

time: 572 us -> 99.4 us (0.17)
  waiting for transfers between devices: 293 us -> 0 us
  local copies, waits for them, and re-layouts: 157 us -> 3.2 us
  Pallas kernels: 0 us -> 93.8 us
  other arithmetic: 38.8 us -> 0.7 us
  loops' own time: 31.5 us -> 0 us
  between operations: 18.2 us -> 1.53 us
  starting transfers between devices: 16 us -> 0 us
  matrix products: 15.1 us -> 0 us
    psum x4 -> x0, waiting for transfers between devices: 245 us -> none  [the longest x2 167 us: body(): lax.psum(probe_step, ('tile', 'scan')) / math.sqrt(total_scans)]
    pallas_call x0 -> x5, Pallas kernels: none -> 93.8 us  [the longest x2 62.2 us: merge(): pl.pallas_call(functools.partial(merge_kernel, n_tile, n_scan, scale, las...]
    dynamic_update_slice x8 -> x0, local copies, waits for them, and re-layouts: 67.1 us -> none  [add_slot(): lax.dynamic_update_slice(accum, current + object_step[slot], (root, row_s...]
    ppermute x4 -> x0, waiting for transfers between devices: 48.2 us -> none  [from_behind(): return lax.ppermute(shard, axis, pairs)]
    another operation x4 -> x0, loops' own time: 31.5 us -> none  [the longest x2 31.3 us: body(): lax.fori_loop(0, slot_count, add_slot, jnp.zeros(padded.shape, jnp.float32))]
    gather x24 -> x0, local copies, waits for them, and re-layouts: 25.9 us -> none
    transpose x4 -> x0, local copies, waits for them, and re-layouts: 23.1 us -> none  [transform(): sectioned.transpose(0, 2, 1, 3).reshape(number, wave_size, 2 * wave_size)]
    reshape x8 -> x0, local copies, waits for them, and re-layouts: 18.8 us -> none  [the longest x4 10.1 us: transform(): sectioned.transpose(0, 2, 1, 3).reshape(number, wave_size, 2 * wave_size)]
  transfers between devices with their start and end apart: 8 -> 0, of which waited for: 7 -> 0; matrix products, arithmetic and copies ran while one was open for 3% -> 0% of each run, Pallas kernels for 0% -> 0%
where the time goes in v1:
time: 99.4 us; the launch traced here: 99.2 us
  Pallas kernels  93.8 us (94%)
  local copies, waits for them, and re-layouts  3.2 us (3%)
  between operations  1.53 us (2%)
    pallas_call x2, Pallas kernels, merge(): pl.pallas_call(functools.partial(merge_kernel, n_tile, n_scan, scale, las...  62.2 us
    pallas_call x2, Pallas kernels, scan_terms(): pl.pallas_call(scan_kernel, out_shape=(jax.ShapeDtypeStruct(padded.shape,...  16.8 us
    pallas_call x1, Pallas kernels, first_rim(): pl.pallas_call(functools.partial(rim_kernel, n_tile, n_scan, wave, parts)...  14.8 us
    unnamed x12, local copies, waits for them, and re-layouts  3.1 us

profile of v1, /device:TPU:0, one launch (start us, length us, event | category | flops | bytes accessed | tf_op | source)
XLA Modules:
  0.0 99.2 jit_solution(2545299623583786191)
XLA Ops:
  0.6 0.0 copy-start.2
  0.6 0.0 copy-start.3
  0.7 0.0 copy-start
  0.7 0.0 copy-start.1
  1.5 0.7 add_bitcast_fusion
  2.2 0.1 copy.11.starts
  2.3 0.0 copy-start.4
  2.3 1.3 %copy-done.4 = f32[2,384,384]{2,1,0:T(8,128)S(1)} copy-done((f32[2,384,384]{2,1,0:T(8,128)S(1)}, f32[2,384,384]{2,1,0:T(8,128)}, u32[]{:S(2)}) %copy-start.4) | copy-done | bytes 1179672
  3.5 14.8 %first_rim.1.padded.old = f32[2,640,384]{2,1,0:T(8,128)S(1)} custom-call(f32[2,384,384]{2,1,0:T(8,128)S(1)} %copy-done.4), custom_call_target="tpu_custom_call" | custom-call | tf_op jit(solution)/shard_map/first_rim/pallas_call | solution.py:438
  18.3 0.0 copy-done.2
  18.3 0.0 copy-done.3
  18.4 0.0 copy-done
  18.4 0.0 copy-done.1
  18.4 8.4 %scan_terms.2 = (f32[2,640,384]{2,1,0:T(8,128)S(1)}, f32[2,256,256]{2,1,0:T(8,128)S(1)}) custom-call(s32[4,2]{1,0:T(4,128)S(1)} %copy.11.starts, s32[1]{0:T(128)} %bitcast.4.counts, f32[2,640,384]{2,1,0:T(8,128)S(1)} %first_rim.1.padded.old, f32[2,256,256]{2,1,0:T(8,128)S(1)} %copy-done, bf16[4,256,256]{2,1,0:T(8,128)(2,1)S(1)} %bitcast.6, ...), custom_call_target="tpu_custom_call" | custom-call | tf_op jit(solution)/shard_map/scan_terms/pallas_call | solution.py:145
  26.8 31.0 %merge.1 = (f32[2,640,384]{2,1,0:T(8,128)S(1)}, f32[2,256,256]{2,1,0:T(8,128)S(1)}) custom-call(f32[2,640,384]{2,1,0:T(8,128)S(1)} %get-tuple-element.8.grad, f32[2,256,256]{2,1,0:T(8,128)S(1)} %get-tuple-element.9.probe_grad, f32[2,640,384]{2,1,0:T(8,128)S(1)} %first_rim.1.padded.old, f32[2,256,256]{2,1,0:T(8,128)S(1)} %copy-done), custom_call_target="tpu_custom_call" | custom-call | tf_op jit(solution)/shard_map/merge/pallas_call | solution.py:461
  57.8 8.4 %scan_terms.3 = (f32[2,640,384]{2,1,0:T(8,128)S(1)}, f32[2,256,256]{2,1,0:T(8,128)S(1)}) custom-call(s32[4,2]{1,0:T(4,128)S(1)} %copy.11.starts, s32[1]{0:T(128)} %bitcast.5.counts, f32[2,640,384]{2,1,0:T(8,128)S(1)} %get-tuple-element.10.padded.old, f32[2,256,256]{2,1,0:T(8,128)S(1)} %get-tuple-element.11.probe, bf16[4,256,256]{2,1,0:T(8,128)(2,1)S(1)} %bitcast.7, ...), custom_call_target="tpu_custom_call" | custom-call | tf_op jit(solution)/shard_map/scan_terms/pallas_call | solution.py:145
  66.3 31.1 %merge_last.1 = (f32[2,384,384]{2,1,0:T(8,128)S(1)}, f32[2,256,256]{2,1,0:T(8,128)S(1)}) custom-call(f32[2,640,384]{2,1,0:T(8,128)S(1)} %get-tuple-element.12.grad, f32[2,256,256]{2,1,0:T(8,128)S(1)} %get-tuple-element.13.probe_grad, f32[2,640,384]{2,1,0:T(8,128)S(1)} %get-tuple-element.10.padded.old, f32[2,256,256]{2,1,0:T(8,128)S(1)} %get-tuple-element.11.probe), custom_call_target="tpu_custom_call" | custom-call | tf_op jit(solution)/shard_map/merge_last/pallas_call | solution.py:461
  97.4 1.0 %copy.15 = f32[2,384,384]{2,1,0:T(8,128)} copy(f32[2,384,384]{2,1,0:T(8,128)S(1)} %get-tuple-element.16) | data formatting | bytes 2359296
  98.4 0.8 copy.16
Async XLA Ops:
  0.6 17.7 %copy-start.2 = (bf16[512,512]{1,0:T(8,128)(2,1)S(1)}, bf16[512,512]{1,0:T(8,128)(2,1)}, u32[]{:S(2)}) copy-start(bf16[512,512]{1,0:T(8,128)(2,1)} %constant.5.clone.table_b) | copy-start | bytes 1572868
  0.6 17.7 %copy-start.3 = (bf16[512,512]{1,0:T(8,128)(2,1)S(1)}, bf16[512,512]{1,0:T(8,128)(2,1)}, u32[]{:S(2)}) copy-start(bf16[512,512]{1,0:T(8,128)(2,1)} %constant.4.clone.table_a) | copy-start | bytes 1572868
  0.7 17.7 %copy-start = (f32[2,256,256]{2,1,0:T(8,128)S(1)}, f32[2,256,256]{2,1,0:T(8,128)}, u32[]{:S(2)}) copy-start(f32[2,256,256]{2,1,0:T(8,128)} %probe.3) | copy-start | bytes 1572868
  0.7 17.7 %copy-start.1 = (bf16[1,1,4,256,256]{4,3,2,1,0:T(8,128)(2,1)S(1)}, bf16[1,1,4,256,256]{4,3,2,1,0:T(8,128)(2,1)}, u32[]{:S(2)}) copy-start(bf16[1,1,4,256,256]{4,3,2,1,0:T(8,128)(2,1)} %param.10) | copy-start | bytes 1572868
  2.3 1.3 %copy-start.4 = (f32[2,384,384]{2,1,0:T(8,128)S(1)}, f32[2,384,384]{2,1,0:T(8,128)}, u32[]{:S(2)}) copy-start(f32[2,384,384]{2,1,0:T(8,128)} %own.1) | copy-start | bytes 3538948

commit v2 on v1

--- a/solution.py
+++ b/solution.py
@@ -27,10 +27,10 @@
 
 
 def scan_kernel(
-    starts, counts, padded, probe, amps, table_a, table_b, grad, probe_grad,
+    anchors, jitter, counts, padded, probe, amps, table_a, table_b, grad, probe_grad,
     window, terms, patch, waves, sections, field,
 ):
-    slots, wave, _ = amps.shape
+    slots, wave = amps.shape[2:4]
     columns = padded.shape[2]
     pieces = columns // LANES
     wide = wave // LANES
@@ -46,9 +46,9 @@
         return jnp.dot(left, right, preferred_element_type=jnp.float32)
 
     def slot_step(slot, carry):
-        row = starts[slot, 0]
-        col = starts[slot, 1]
-        live = jnp.where(slot < counts[0], 1.0, 0.0).astype(jnp.float32)
+        row = anchors[0, 0, slot, 0] + jitter[0, 0, slot, 0]
+        col = anchors[0, 0, slot, 1] + jitter[0, 0, slot, 1]
+        live = jnp.where(slot < counts[0, 0], 1.0, 0.0).astype(jnp.float32)
         back = lax.rem(LANES - lax.rem(col, LANES), LANES)
         ahead = lax.rem(col, LANES)
         skip = lax.div(col, LANES)
@@ -92,7 +92,7 @@
             real = field[top : top + CHUNK, :wave]
             imag = field[top : top + CHUNK, wave:]
             power = real * real + imag * imag
-            measured = amps[slot, top : top + CHUNK, :].astype(jnp.float32)
+            measured = amps[0, 0, slot, top : top + CHUNK, :].astype(jnp.float32)
             factor = (measured * lax.rsqrt(power + 0.25) - 1.0) * live
             waves[top : top + CHUNK, :] = (real * factor).astype(jnp.bfloat16)
             waves[wave + top : wave + top + CHUNK, :] = (imag * factor).astype(jnp.bfloat16)
@@ -136,8 +136,8 @@
             grad[part, :, p * LANES : (p + 1) * LANES] = terms[part, p]
 
 
-def scan_terms(starts, counts, padded, probe, amps, table_a, table_b):
-    slots, wave, _ = amps.shape
+def scan_terms(anchors, jitter, counts, padded, probe, amps, table_a, table_b):
+    wave = amps.shape[3]
     _, extent, columns = padded.shape
     blocks = pltpu.VMEM((2, columns // LANES, extent, LANES), jnp.float32)
     vmem = pl.BlockSpec(memory_space=pltpu.VMEM)
@@ -148,7 +148,7 @@
             jax.ShapeDtypeStruct(padded.shape, jnp.float32),
             jax.ShapeDtypeStruct(probe.shape, jnp.float32),
         ),
-        in_specs=[smem, smem, vmem, vmem, vmem, vmem, vmem],
+        in_specs=[smem, smem, smem, vmem, vmem, vmem, vmem, vmem],
         out_specs=(vmem, vmem),
         scratch_shapes=[
             blocks,
@@ -160,7 +160,7 @@
         ],
         compiler_params=pltpu.CompilerParams(vmem_limit_bytes=32 * 1024 * 1024),
         name="scan_terms",
-    )(starts, counts, padded, probe, amps, table_a, table_b)
+    )(anchors, jitter, counts, padded, probe, amps, table_a, table_b)
 
 
 class Links:
@@ -226,15 +226,14 @@
         pl.when(when)(action)
 
 
-def rim_kernel(n_tile, n_scan, wave, parts, own, padded, send, recv):
+def rim_kernel(n_tile, n_scan, wave, parts, own, padded, send, recv, stay):
     links = Links(send, recv, n_tile, n_scan)
     rows = own.shape[1]
     chips, tile, core, chip = links.chips, links.tile, links.core, links.chip
     share = wave // chips
     some = share // parts
     above, below = tile > 0, tile < n_tile - 1
-    tiles = sorted({1, n_tile - 1})
-    links.greet(tiles)
+    links.greet(sorted({1, n_tile - 1}))
 
     def at(owner, part, base):
         return pl.ds(base + owner * share + part * some, some)
@@ -244,7 +243,8 @@
         links.copy(own.at[core, at(chip, p, 0)], padded.at[core, at(chip, p, rows)], up, above)
         for p in range(parts)
     ]
-    padded[:, :rows, :] = own[...]
+    local = pltpu.make_async_copy(own, padded.at[:, pl.ds(0, rows)], stay)
+    local.start()
 
     @pl.when(tile == n_tile - 1)
     def _():
@@ -263,20 +263,21 @@
         landed.append(links.copy(here, here, links.other_core(), below))
     for made in landed:
         on(below, made.wait_recv)
+    local.wait()
     links.finish()
 
 
 def merge_kernel(
-    n_tile, n_scan, scale, last, grad, probe_grad, old, probe, out, probe_out,
-    core_in, core_probe, total, probe_total, rim_in, head_in, tail_in, probe_in,
-    rim_sum, rim_back, probe_parts, send, recv,
+    n_tile, n_scan, parts, scale, last, grad, probe_grad, old, probe, out, probe_out,
+    core_in, core_probe, total, probe_total, chip_in, probe_in, rim_back, probe_parts,
+    send, recv,
 ):
     links = Links(send, recv, n_tile, n_scan)
     chips, tile, core, chip = links.chips, links.tile, links.core, links.chip
     wave = probe.shape[1]
     rows = grad.shape[1] - wave
     rest = rows - wave
-    head, tail = wave // chips, rest // chips
+    head, some = wave // chips, wave // parts
     owners = probe_parts_of(n_tile, chips, wave)
     fine = head // owners
     above, below = tile > 0, tile < n_tile - 1
@@ -285,79 +286,80 @@
     links.greet(range(1, n_tile))
     other = 1 - core
     partner = links.other_core()
-
-    def to_core(first, count):
-        span = pl.ds(first, count)
+    others = range(1, chips)
+    spans = [pl.ds(p * some, some) for p in range(parts)]
+    rims = [pl.ds(rows + p * some, some) for p in range(parts)]
+
+    def to_core(span):
         return links.copy(grad.at[other, span], core_in.at[span], partner)
 
-    got_rim = to_core(rows, wave)
     got_probe = links.copy(probe_grad.at[other], core_probe, partner)
-    got_head = to_core(0, wave)
-    got_tail = to_core(wave, rest)
-
-    def fold(got, first, count, share, landing):
-        got.wait_recv()
-        span = pl.ds(first, count)
-        total[span, :] = grad[core, span, :] + core_in[span, :]
-        sent = []
-        for k in range(1, chips):
-            piece = total.at[pl.ds(first + links.chip_at(k) * share, share)]
-            sent.append(links.copy(piece, landing.at[chip], links.on_chip(k)))
-        return sent
-
-    def gathered(sent, mine, landing):
-        for made in sent:
-            made.wait_recv()
-        for k in range(1, chips):
-            mine = mine + landing[links.chip_at(k)]
-        return mine
-
-    rim_sent = fold(got_rim, rows, wave, head, rim_in)
+    got_rims = [to_core(span) for span in rims]
+    got_tail = to_core(pl.ds(wave, rest))
+    got_head = to_core(pl.ds(0, wave))
+
     got_probe.wait_recv()
     probe_total[...] = probe_grad[core] + core_probe[...]
     probe_sent = []
-    for k in range(1, chips):
+    for k in others:
         piece = probe_total.at[pl.ds(links.chip_at(k) * head, head)]
         probe_sent.append(links.copy(piece, probe_in.at[chip], links.on_chip(k)))
-    head_sent = fold(got_head, 0, wave, head, head_in)
-    tail_sent = fold(got_tail, wave, rest, tail, tail_in)
+
+    rims_sent = []
+    for got, span, landing in zip(got_rims, rims, spans):
+        got.wait_recv()
+        total[span, :] = grad[core, span, :] + core_in[span, :]
+        rims_sent.append(links.copy(total.at[span], rim_back.at[landing], down, below))
+
+    def to_chips(span):
+        return [
+            links.copy(total.at[span], chip_in.at[chip, span], links.on_chip(k)) for k in others
+        ]
+
+    tail_rows = pl.ds(wave, rest)
+    got_tail.wait_recv()
+    total[tail_rows, :] = grad[core, tail_rows, :] + core_in[tail_rows, :]
+    tail_sent = to_chips(tail_rows)
 
     inverse = RATE / (
         jnp.max(probe[0] * probe[0] + probe[1] * probe[1], axis=(0, 1), keepdims=True) + 1e-06
     )
-
-    rim_sum[...] = gathered(rim_sent, total[pl.ds(rows + chip * head, head), :], rim_in)
-    rim_sent = links.copy(rim_sum, rim_back, down, below)
-
-    mine = gathered(probe_sent, probe_total[pl.ds(chip * head, head), :], probe_in)
-    probe_total[pl.ds(chip * head, head), :] = mine
+    got_head.wait_recv()
 
     def owns(index):
         return None if owners == n_tile else index < owners
 
-    spread = []
-    for k in range(1, n_tile):
-        to = (tile + k) % n_tile
-        piece = jnp.minimum(to, owners - 1) if owners < n_tile else to
-        spread.append(
-            links.copy(
-                probe_total.at[pl.ds(chip * head + piece * fine, fine)],
-                probe_parts.at[tile],
-                {"tile": to},
-                owns(to),
-            )
-        )
-
-    own_part = jnp.minimum(tile, owners - 1) if owners < n_tile else tile
-    own_rows = pl.ds(chip * head + own_part * fine, fine)
+    def owned(index):
+        return index if owners == n_tile else jnp.minimum(index, owners - 1)
+
+    head_sent, spread = [], []
+    for p, (span, made) in enumerate(zip(spans, rims_sent)):
+        on(above, made.wait_recv)
+        back = jnp.where(above, rim_back[span, :], 0.0)
+        total[span, :] = grad[core, span, :] + core_in[span, :] + back
+        head_sent.append(to_chips(span))
+        if p == 0:
+            for made in probe_sent:
+                made.wait_recv()
+            mine = pl.ds(chip * head, head)
+            whole = probe_total[mine, :]
+            for k in others:
+                whole = whole + probe_in[links.chip_at(k)]
+            probe_total[mine, :] = whole
+            for k in range(1, n_tile):
+                to = (tile + k) % n_tile
+                piece = probe_total.at[pl.ds(chip * head + owned(to) * fine, fine)]
+                spread.append(links.copy(piece, probe_parts.at[tile], {"tile": to}, owns(to)))
+
+    own_rows = pl.ds(chip * head + owned(tile) * fine, fine)
     for made in spread:
         on(owns(tile), made.wait_recv)
 
     def close():
-        sum_here = probe_total[own_rows, :]
+        whole = probe_total[own_rows, :]
         for k in range(1, n_tile):
-            sum_here = sum_here + probe_parts[(tile + k) % n_tile]
-        probe_out[core, own_rows, :] = probe[core, own_rows, :] + sum_here * scale
+            whole = whole + probe_parts[(tile + k) % n_tile]
+        probe_out[core, own_rows, :] = probe[core, own_rows, :] + whole * scale
 
     on(owns(tile), close)
     place = probe_out.at[core, own_rows]
@@ -365,59 +367,50 @@
         links.copy(place, place, {"tile": (tile + k) % n_tile}, owns(tile))
         for k in range(1, n_tile)
     ]
-
-    head_rows = pl.ds(chip * head, head)
-    head_sum = gathered(head_sent, total[head_rows, :], head_in)
-    on(above, rim_sent.wait_recv)
-    back = jnp.where(above, rim_back[...], 0.0)
-    out[core, head_rows, :] = old[core, head_rows, :] + inverse * (head_sum + back)
-    here = out.at[core, head_rows]
-    head_across = [links.copy(here, here, links.on_chip(k)) for k in range(1, chips)]
-    rims = []
-    if not last:
-        rims.append(links.copy(here, out.at[core, pl.ds(rows + chip * head, head)], up, above))
-    core_last = [(links.copy(here, here, partner), None)]
-
-    tail_rows = pl.ds(wave + chip * tail, tail)
-    tail_sum = gathered(tail_sent, total[tail_rows, :], tail_in)
-    out[core, tail_rows, :] = old[core, tail_rows, :] + inverse * tail_sum
-    here = out.at[core, tail_rows]
-    tail_across = [links.copy(here, here, links.on_chip(k)) for k in range(1, chips)]
-    core_last.append((links.copy(here, here, partner), None))
+    landed = []
+
+    def update(span, sent):
+        for made in sent:
+            made.wait_recv()
+        if chips == 2:
+            whole = total[span, :] + chip_in[1 - chip, span, :]
+        else:
+            whole = None
+            for k in range(chips):
+                term = jnp.where(chip == k, total[span, :], chip_in[k, span, :])
+                whole = term if whole is None else whole + term
+        out[core, span, :] = old[core, span, :] + inverse * whole
+        here = out.at[core, span]
+        landed.append((links.copy(here, here, partner), None))
+
+    update(tail_rows, tail_sent)
 
     for k, made in zip(range(1, n_tile), probe_back):
         on(owns((tile + n_tile - k) % n_tile), made.wait_recv)
     here = probe_out.at[core, pl.ds(chip * head, head)]
-    probe_across = [links.copy(here, here, links.on_chip(k)) for k in range(1, chips)]
-    core_last.append((links.copy(here, here, partner), None))
-
-    for k in range(1, chips):
-        head_across[k - 1].wait_recv()
-        begin = links.chip_at(chips - k) * head
-        here = out.at[core, pl.ds(begin, head)]
+    probe_across = [links.copy(here, here, links.on_chip(k)) for k in others]
+    landed.append((links.copy(here, here, partner), None))
+
+    rims_back = []
+    for span, rim, sent in zip(spans, rims, head_sent):
+        update(span, sent)
         if not last:
-            rims.append(links.copy(here, out.at[core, pl.ds(rows + begin, head)], up, above))
-        core_last.append((links.copy(here, here, partner), None))
-    for k in range(1, chips):
-        tail_across[k - 1].wait_recv()
-        here = out.at[core, pl.ds(wave + links.chip_at(chips - k) * tail, tail)]
-        core_last.append((links.copy(here, here, partner), None))
-    for k in range(1, chips):
+            rims_back.append(links.copy(out.at[core, span], out.at[core, rim], up, above))
+    for k in others:
         probe_across[k - 1].wait_recv()
         here = probe_out.at[core, pl.ds(links.chip_at(chips - k) * head, head)]
-        core_last.append((links.copy(here, here, partner), None))
+        landed.append((links.copy(here, here, partner), None))
     if not last:
 
         @pl.when(tile == n_tile - 1)
         def _():
             out[:, rows:, :] = jnp.zeros((2, wave, out.shape[2]), jnp.float32)
 
-        for k, made in enumerate(rims):
+        for rim, made in zip(rims, rims_back):
             on(below, made.wait_recv)
-            begin = links.chip_at((chips - k) % chips) * head
-            here = out.at[core, pl.ds(rows + begin, head)]
-            core_last.append((links.copy(here, here, partner, below), below))
-    for made, when in core_last:
+            here = out.at[core, rim]
+            landed.append((links.copy(here, here, partner, below), below))
+    for made, when in landed:
         on(when, made.wait_recv)
     links.finish()
 
@@ -433,14 +426,18 @@
     n_tile, n_scan = lax.axis_size("tile"), lax.axis_size("scan")
     _, rows, columns = own.shape
     vmem = pl.BlockSpec(memory_space=pltpu.VMEM)
-    parts = 2
+    parts = 4
     copies = parts * (2 * (n_scan // CORES) + 1)
     return pl.pallas_call(
         functools.partial(rim_kernel, n_tile, n_scan, wave, parts),
         out_shape=jax.ShapeDtypeStruct((2, rows + wave, columns), jnp.float32),
-        in_specs=[vmem],
+        in_specs=[pl.BlockSpec(memory_space=pltpu.HBM)],
         out_specs=vmem,
-        scratch_shapes=[pltpu.SemaphoreType.DMA((copies,)), pltpu.SemaphoreType.DMA((copies,))],
+        scratch_shapes=[
+            pltpu.SemaphoreType.DMA((copies,)),
+            pltpu.SemaphoreType.DMA((copies,)),
+            pltpu.SemaphoreType.DMA,
+        ],
         compiler_params=pltpu.CompilerParams(
             collective_id=0, has_side_effects=True, vmem_limit_bytes=24 * 1024 * 1024
         ),
@@ -454,12 +451,13 @@
     _, wave, _ = probe.shape
     _, extent, columns = grad.shape
     rows = extent - wave
-    head, tail = wave // chips, (rows - wave) // chips
+    head = wave // chips
     fine = head // probe_parts_of(n_tile, chips, wave)
     vmem = pl.BlockSpec(memory_space=pltpu.VMEM)
-    copies = 16 + 10 * chips + 2 * n_tile
+    parts = 4
+    copies = 8 + (5 + parts) * chips + 2 * n_tile + 5 * parts
     return pl.pallas_call(
-        functools.partial(merge_kernel, n_tile, n_scan, scale, last),
+        functools.partial(merge_kernel, n_tile, n_scan, parts, scale, last),
         out_shape=(
             jax.ShapeDtypeStruct((2, rows if last else extent, columns), jnp.float32),
             jax.ShapeDtypeStruct(probe.shape, jnp.float32),
@@ -471,12 +469,9 @@
             pltpu.VMEM((wave, wave), jnp.float32),
             pltpu.VMEM((extent, columns), jnp.float32),
             pltpu.VMEM((wave, wave), jnp.float32),
-            pltpu.VMEM((chips, head, columns), jnp.float32),
-            pltpu.VMEM((chips, head, columns), jnp.float32),
-            pltpu.VMEM((chips, tail, columns), jnp.float32),
+            pltpu.VMEM((chips, rows, columns), jnp.float32),
             pltpu.VMEM((chips, head, wave), jnp.float32),
-            pltpu.VMEM((head, columns), jnp.float32),
-            pltpu.VMEM((head, columns), jnp.float32),
+            pltpu.VMEM((wave, columns), jnp.float32),
             pltpu.VMEM((n_tile, fine, wave), jnp.float32),
             pltpu.SemaphoreType.DMA((copies,)),
             pltpu.SemaphoreType.DMA((copies,)),
@@ -492,8 +487,6 @@
     wave = probe_field.shape[1]
     slots = amplitudes.shape[2]
     table_a, table_b = tables(wave)
-    starts = (anchors + jitter)[0, 0]
-    measured = amplitudes[0, 0]
     total_scans = slots * lax.axis_size("tile") * lax.axis_size("scan")
     scale = 1.0 / math.sqrt(total_scans)
     padded = first_rim(object_field, wave)
@@ -501,7 +494,7 @@
     for iteration in range(ITERS):
         last = iteration == ITERS - 1
         grad, probe_grad = scan_terms(
-            starts, counts[0], padded, probe, measured, table_a, table_b
+            anchors, jitter, counts, padded, probe, amplitudes, table_a, table_b
         )
         padded, probe = merge(grad, probe_grad, padded, probe, scale, last, 1 + iteration)
     return (padded, probe)

time: 99.4 us -> 95.8 us (0.964)
  Pallas kernels: 93.8 us -> 89.4 us
  local copies, waits for them, and re-layouts: 3.2 us -> 4.63 us
    pallas_call x2, Pallas kernels: 62.2 us -> 58.4 us  [merge(): pl.pallas_call(functools.partial(merge_kernel, n_tile, n_scan, parts, sca...]
    unnamed x12 -> x14, local copies, waits for them, and re-layouts: 3.1 us -> 4.63 us
where the time goes in v2:
time: 95.8 us; the launch traced here: 95.6 us
  Pallas kernels  89.4 us (93%)
  local copies, waits for them, and re-layouts  4.63 us (5%)
  between operations  1.52 us (2%)
    pallas_call x2, Pallas kernels, merge(): pl.pallas_call(functools.partial(merge_kernel, n_tile, n_scan, parts, sca...  58.4 us
    pallas_call x2, Pallas kernels, scan_terms(): pl.pallas_call(scan_kernel, out_shape=(jax.ShapeDtypeStruct(padded.shape,...  16.9 us
    pallas_call x1, Pallas kernels, first_rim(): pl.pallas_call(functools.partial(rim_kernel, n_tile, n_scan, wave, parts)...  14.1 us
    unnamed x14, local copies, waits for them, and re-layouts  4.63 us

profile of v2, /device:TPU:0, one launch (start us, length us, event | category | flops | bytes accessed | tf_op | source)
XLA Modules:
  0.0 95.6 jit_solution(12688837604654557372)
XLA Ops:
  0.6 0.0 copy-start.2
  0.6 0.0 copy-start.3
  0.7 0.0 copy-start.1
  0.7 0.0 copy-start
  1.5 0.8 copy.12.anchors
  2.2 0.8 copy.13.jitter
  3.0 0.0 copy-start.4
  3.0 1.3 %copy-done.4 = f32[2,384,384]{2,1,0:T(8,128)S(1)} copy-done((f32[2,384,384]{2,1,0:T(8,128)S(1)}, f32[2,384,384]{2,1,0:T(8,128)}, u32[]{:S(2)}) %copy-start.4) | copy-done | bytes 1179672
  4.3 14.1 %first_rim.1.padded.old = f32[2,640,384]{2,1,0:T(8,128)S(1)} custom-call(f32[2,384,384]{2,1,0:T(8,128)S(1)} %copy-done.4), custom_call_target="tpu_custom_call" | custom-call | tf_op jit(solution)/shard_map/first_rim/pallas_call | solution.py:431
  18.4 0.0 copy-done.2
  18.4 0.0 copy-done.3
  18.4 0.0 copy-done.1
  18.4 0.0 copy-done
  18.4 8.5 %scan_terms.2 = (f32[2,640,384]{2,1,0:T(8,128)S(1)}, f32[2,256,256]{2,1,0:T(8,128)S(1)}) custom-call(s32[1,1,4,2]{3,2,1,0:T(4,128)S(1)} %copy.12.anchors, s32[1,1,4,2]{3,2,1,0:T(4,128)S(1)} %copy.13.jitter, s32[1,1]{1,0:T(1,128)S(6)} %copy.16.counts, f32[2,640,384]{2,1,0:T(8,128)S(1)} %first_rim.1.padded.old, f32[2,256,256]{2,1,0:T(8,128)S(1)} %copy-done, ...), custom_call_target="tpu_custom_call" | custom-call | tf_op jit(solution)/shard_map/scan_terms/pallas_call | solution.py:145
  26.9 32.1 %merge.1 = (f32[2,640,384]{2,1,0:T(8,128)S(1)}, f32[2,256,256]{2,1,0:T(8,128)S(1)}) custom-call(f32[2,640,384]{2,1,0:T(8,128)S(1)} %get-tuple-element.8.grad, f32[2,256,256]{2,1,0:T(8,128)S(1)} %get-tuple-element.9.probe_grad, f32[2,640,384]{2,1,0:T(8,128)S(1)} %first_rim.1.padded.old, f32[2,256,256]{2,1,0:T(8,128)S(1)} %copy-done), custom_call_target="tpu_custom_call" | custom-call | tf_op jit(solution)/shard_map/merge/pallas_call | solution.py:459
  59.0 8.5 %scan_terms.3 = (f32[2,640,384]{2,1,0:T(8,128)S(1)}, f32[2,256,256]{2,1,0:T(8,128)S(1)}) custom-call(s32[1,1,4,2]{3,2,1,0:T(4,128)S(1)} %copy.12.anchors, s32[1,1,4,2]{3,2,1,0:T(4,128)S(1)} %copy.13.jitter, s32[1,1]{1,0:T(1,128)S(6)} %copy.16.counts, f32[2,640,384]{2,1,0:T(8,128)S(1)} %get-tuple-element.10.padded.old, ...), custom_call_target="tpu_custom_call" | custom-call | tf_op jit(solution)/shard_map/scan_terms/pallas_call | solution.py:145
  67.5 26.3 %merge_last.1 = (f32[2,384,384]{2,1,0:T(8,128)S(1)}, f32[2,256,256]{2,1,0:T(8,128)S(1)}) custom-call(f32[2,640,384]{2,1,0:T(8,128)S(1)} %get-tuple-element.12.grad, f32[2,256,256]{2,1,0:T(8,128)S(1)} %get-tuple-element.13.probe_grad, f32[2,640,384]{2,1,0:T(8,128)S(1)} %get-tuple-element.10.padded.old, f32[2,256,256]{2,1,0:T(8,128)S(1)} %get-tuple-element.11.probe), custom_call_target="tpu_custom_call" | custom-call | tf_op jit(solution)/shard_map/merge_last/pallas_call | solution.py:459
  93.8 1.0 %copy.17 = f32[2,384,384]{2,1,0:T(8,128)} copy(f32[2,384,384]{2,1,0:T(8,128)S(1)} %get-tuple-element.16) | data formatting | bytes 2359296
  94.8 0.8 copy.18
Async XLA Ops:
  0.6 17.8 %copy-start.2 = (bf16[512,512]{1,0:T(8,128)(2,1)S(1)}, bf16[512,512]{1,0:T(8,128)(2,1)}, u32[]{:S(2)}) copy-start(bf16[512,512]{1,0:T(8,128)(2,1)} %constant.5.clone.table_b) | copy-start | bytes 1572868
  0.6 17.8 %copy-start.3 = (bf16[512,512]{1,0:T(8,128)(2,1)S(1)}, bf16[512,512]{1,0:T(8,128)(2,1)}, u32[]{:S(2)}) copy-start(bf16[512,512]{1,0:T(8,128)(2,1)} %constant.4.clone.table_a) | copy-start | bytes 1572868
  0.7 17.8 %copy-start.1 = (bf16[1,1,4,256,256]{4,3,2,1,0:T(8,128)(2,1)S(1)}, bf16[1,1,4,256,256]{4,3,2,1,0:T(8,128)(2,1)}, u32[]{:S(2)}) copy-start(bf16[1,1,4,256,256]{4,3,2,1,0:T(8,128)(2,1)} %amps.3) | copy-start | bytes 1572868
  0.7 17.8 %copy-start = (f32[2,256,256]{2,1,0:T(8,128)S(1)}, f32[2,256,256]{2,1,0:T(8,128)}, u32[]{:S(2)}) copy-start(f32[2,256,256]{2,1,0:T(8,128)} %probe.3) | copy-start | bytes 1572868
  3.0 1.3 %copy-start.4 = (f32[2,384,384]{2,1,0:T(8,128)S(1)}, f32[2,384,384]{2,1,0:T(8,128)}, u32[]{:S(2)}) copy-start(f32[2,384,384]{2,1,0:T(8,128)} %own.1) | copy-start | bytes 3538948

commit v3 on v2

--- a/solution.py
+++ b/solution.py
@@ -27,8 +27,8 @@
 
 
 def scan_kernel(
-    anchors, jitter, counts, padded, probe, amps, table_a, table_b, grad, probe_grad,
-    window, terms, patch, waves, sections, field,
+    starts, counts, padded, probe, amps, table_a, table_b, grad, probe_grad,
+    window, terms, patches, waves_all, sections_all, fields,
 ):
     slots, wave = amps.shape[2:4]
     columns = padded.shape[2]
@@ -45,15 +45,16 @@
     def dot(left, right):
         return jnp.dot(left, right, preferred_element_type=jnp.float32)
 
-    def slot_step(slot, carry):
-        row = anchors[0, 0, slot, 0] + jitter[0, 0, slot, 0]
-        col = anchors[0, 0, slot, 1] + jitter[0, 0, slot, 1]
+    def slot_step(slot):
+        patch, waves = patches.at[slot], waves_all.at[slot]
+        sections, field = sections_all.at[slot], fields.at[slot]
+        row = starts[slot, 0]
+        col = starts[slot, 1]
         live = jnp.where(slot < counts[0, 0], 1.0, 0.0).astype(jnp.float32)
-        back = lax.rem(LANES - lax.rem(col, LANES), LANES)
+        back = lax.rem(LANES - col, LANES)
         ahead = lax.rem(col, LANES)
-        skip = lax.div(col, LANES)
-        low = lane < LANES - ahead
-        high = lane >= ahead
+        low = lane < LANES - col
+        high = lane >= col
 
         for top in range(0, wave, CHUNK):
             halves = []
@@ -64,14 +65,7 @@
                     )
                     for p in range(pieces)
                 ]
-                turned.append(turned[-1])
-                lanes_out = []
-                for w in range(wide):
-                    best = None
-                    for k in range(pieces - wide + 1):
-                        this = jnp.where(low, turned[w + k], turned[w + k + 1])
-                        best = this if best is None else jnp.where(skip == k, this, best)
-                    lanes_out.append(best)
+                lanes_out = [jnp.where(low, turned[w], turned[w + 1]) for w in range(wide)]
                 halves.append(jnp.concatenate(lanes_out, 1))
             real, imag = halves
             patch[0, top : top + CHUNK, :] = real
@@ -83,10 +77,12 @@
                 jnp.bfloat16
             )
 
+        yield
         sectioned = dot(table_a[...], waves[...]).astype(jnp.bfloat16)
         sections[:, :wave] = sectioned[:wave]
         sections[:, wave:] = sectioned[wave:]
         field[...] = dot(sections[...], table_b[...])
+        yield
 
         for top in range(0, wave, CHUNK):
             real = field[top : top + CHUNK, :wave]
@@ -97,10 +93,12 @@
             waves[top : top + CHUNK, :] = (real * factor).astype(jnp.bfloat16)
             waves[wave + top : wave + top + CHUNK, :] = (imag * factor).astype(jnp.bfloat16)
 
+        yield
         sectioned = dot(table_b[...], waves[...]).astype(jnp.bfloat16)
         sections[:, :wave] = sectioned[:wave]
         sections[:, wave:] = sectioned[wave:]
         field[...] = dot(sections[...], table_a[...])
+        yield
 
         for top in range(0, wave, CHUNK):
             real = field[top : top + CHUNK, :wave]
@@ -118,26 +116,25 @@
                     for w in range(wide)
                 ]
                 zero = jnp.zeros((CHUNK, LANES), jnp.float32)
-
-                def block(index):
-                    return turned[index] if 0 <= index < wide else zero
-
+                ends = [zero] + turned + [zero]
                 for p in range(pieces):
-                    best = None
-                    for k in range(pieces - wide + 1):
-                        this = jnp.where(high, block(p - k), block(p - k - 1))
-                        best = this if best is None else jnp.where(skip == k, this, best)
-                    terms[part, p, pl.ds(row + top, CHUNK), :] += best
-        return carry
-
-    lax.fori_loop(0, slots, slot_step, 0)
+                    terms[part, p, pl.ds(row + top, CHUNK), :] += jnp.where(
+                        high, ends[p + 1], ends[p]
+                    )
+
+    waiting = [slot_step(slot) for slot in range(slots)]
+    active = []
+    while waiting or active:
+        if waiting:
+            active.append(waiting.pop(0))
+        active = [one for one in active if next(one, active) is None]
     for part in range(2):
         for p in range(pieces):
             grad[part, :, p * LANES : (p + 1) * LANES] = terms[part, p]
 
 
-def scan_terms(anchors, jitter, counts, padded, probe, amps, table_a, table_b):
-    wave = amps.shape[3]
+def scan_terms(starts, counts, padded, probe, amps, table_a, table_b):
+    slots, wave = amps.shape[2:4]
     _, extent, columns = padded.shape
     blocks = pltpu.VMEM((2, columns // LANES, extent, LANES), jnp.float32)
     vmem = pl.BlockSpec(memory_space=pltpu.VMEM)
@@ -148,19 +145,19 @@
             jax.ShapeDtypeStruct(padded.shape, jnp.float32),
             jax.ShapeDtypeStruct(probe.shape, jnp.float32),
         ),
-        in_specs=[smem, smem, smem, vmem, vmem, vmem, vmem, vmem],
+        in_specs=[smem, smem, vmem, vmem, vmem, vmem, vmem],
         out_specs=(vmem, vmem),
         scratch_shapes=[
             blocks,
             blocks,
-            pltpu.VMEM((2, wave, wave), jnp.float32),
-            pltpu.VMEM((2 * wave, wave), jnp.bfloat16),
-            pltpu.VMEM((wave, 2 * wave), jnp.bfloat16),
-            pltpu.VMEM((wave, 2 * wave), jnp.float32),
+            pltpu.VMEM((slots, 2, wave, wave), jnp.float32),
+            pltpu.VMEM((slots, 2 * wave, wave), jnp.bfloat16),
+            pltpu.VMEM((slots, wave, 2 * wave), jnp.bfloat16),
+            pltpu.VMEM((slots, wave, 2 * wave), jnp.float32),
         ],
         compiler_params=pltpu.CompilerParams(vmem_limit_bytes=32 * 1024 * 1024),
         name="scan_terms",
-    )(anchors, jitter, counts, padded, probe, amps, table_a, table_b)
+    )(starts, counts, padded, probe, amps, table_a, table_b)
 
 
 class Links:
@@ -319,7 +316,8 @@
     tail_rows = pl.ds(wave, rest)
     got_tail.wait_recv()
     total[tail_rows, :] = grad[core, tail_rows, :] + core_in[tail_rows, :]
-    tail_sent = to_chips(tail_rows)
+    early, late = pl.ds(wave, rest // 2), pl.ds(wave + rest // 2, rest // 2)
+    early_sent = to_chips(early)
 
     inverse = RATE / (
         jnp.max(probe[0] * probe[0] + probe[1] * probe[1], axis=(0, 1), keepdims=True) + 1e-06
@@ -351,6 +349,8 @@
                 piece = probe_total.at[pl.ds(chip * head + owned(to) * fine, fine)]
                 spread.append(links.copy(piece, probe_parts.at[tile], {"tile": to}, owns(to)))
 
+    late_sent = to_chips(late)
+
     own_rows = pl.ds(chip * head + owned(tile) * fine, fine)
     for made in spread:
         on(owns(tile), made.wait_recv)
@@ -383,7 +383,7 @@
         here = out.at[core, span]
         landed.append((links.copy(here, here, partner), None))
 
-    update(tail_rows, tail_sent)
+    update(early, early_sent)
 
     for k, made in zip(range(1, n_tile), probe_back):
         on(owns((tile + n_tile - k) % n_tile), made.wait_recv)
@@ -396,6 +396,7 @@
         update(span, sent)
         if not last:
             rims_back.append(links.copy(out.at[core, span], out.at[core, rim], up, above))
+    update(late, late_sent)
     for k in others:
         probe_across[k - 1].wait_recv()
         here = probe_out.at[core, pl.ds(links.chip_at(chips - k) * head, head)]
@@ -455,7 +456,7 @@
     fine = head // probe_parts_of(n_tile, chips, wave)
     vmem = pl.BlockSpec(memory_space=pltpu.VMEM)
     parts = 4
-    copies = 8 + (5 + parts) * chips + 2 * n_tile + 5 * parts
+    copies = 8 + (6 + parts) * chips + 2 * n_tile + 5 * parts
     return pl.pallas_call(
         functools.partial(merge_kernel, n_tile, n_scan, parts, scale, last),
         out_shape=(
@@ -487,6 +488,7 @@
     wave = probe_field.shape[1]
     slots = amplitudes.shape[2]
     table_a, table_b = tables(wave)
+    starts = (anchors + jitter)[0, 0]
     total_scans = slots * lax.axis_size("tile") * lax.axis_size("scan")
     scale = 1.0 / math.sqrt(total_scans)
     padded = first_rim(object_field, wave)
@@ -494,7 +496,7 @@
     for iteration in range(ITERS):
         last = iteration == ITERS - 1
         grad, probe_grad = scan_terms(
-            anchors, jitter, counts, padded, probe, amplitudes, table_a, table_b
+            starts, counts, padded, probe, amplitudes, table_a, table_b
         )
         padded, probe = merge(grad, probe_grad, padded, probe, scale, last, 1 + iteration)
     return (padded, probe)

time: 95.8 us -> 88.1 us (0.920)
  Pallas kernels: 89.4 us -> 82.5 us
  local copies, waits for them, and re-layouts: 4.63 us -> 3.2 us
    pallas_call x2, Pallas kernels: 16.9 us -> 9.97 us  [scan_terms(): pl.pallas_call(scan_kernel, out_shape=(jax.ShapeDtypeStruct(padded.shape,...]
    unnamed x14 -> x12, local copies, waits for them, and re-layouts: 4.63 us -> 3.1 us
where the time goes in v3:
time: 88.1 us; the launch traced here: 87.9 us
  Pallas kernels  82.5 us (94%)
  local copies, waits for them, and re-layouts  3.2 us (4%)
  between operations  1.53 us (2%)
    pallas_call x2, Pallas kernels, merge(): pl.pallas_call(functools.partial(merge_kernel, n_tile, n_scan, parts, sca...  58.4 us
    pallas_call x1, Pallas kernels, first_rim(): pl.pallas_call(functools.partial(rim_kernel, n_tile, n_scan, wave, parts)...  14.1 us
    pallas_call x2, Pallas kernels, scan_terms(): pl.pallas_call(scan_kernel, out_shape=(jax.ShapeDtypeStruct(padded.shape,...  9.97 us
    unnamed x12, local copies, waits for them, and re-layouts  3.1 us

profile of v3, /device:TPU:0, one launch (start us, length us, event | category | flops | bytes accessed | tf_op | source)
XLA Modules:
  0.0 87.9 jit_solution(1074301043482362378)
XLA Ops:
  0.6 0.0 copy-start.2
  0.6 0.0 copy-start.3
  0.7 0.0 copy-start.1
  0.7 0.0 copy-start
  1.5 0.7 add_bitcast_fusion
  2.2 0.1 copy.11.starts
  2.3 0.0 copy-start.4
  2.3 1.3 %copy-done.4 = f32[2,384,384]{2,1,0:T(8,128)S(1)} copy-done((f32[2,384,384]{2,1,0:T(8,128)S(1)}, f32[2,384,384]{2,1,0:T(8,128)}, u32[]{:S(2)}) %copy-start.4) | copy-done | bytes 1179672
  3.5 14.1 %first_rim.1.padded.old = f32[2,640,384]{2,1,0:T(8,128)S(1)} custom-call(f32[2,384,384]{2,1,0:T(8,128)S(1)} %copy-done.4), custom_call_target="tpu_custom_call" | custom-call | tf_op jit(solution)/shard_map/first_rim/pallas_call | solution.py:432
  17.7 0.0 copy-done.2
  17.7 0.0 copy-done.3
  17.7 0.0 copy-done.1
  17.7 0.0 copy-done
  17.7 5.0 %scan_terms.2 = (f32[2,640,384]{2,1,0:T(8,128)S(1)}, f32[2,256,256]{2,1,0:T(8,128)S(1)}) custom-call(s32[4,2]{1,0:T(4,128)S(1)} %copy.11.starts, s32[1,1]{1,0:T(1,128)S(6)} %copy.14.counts, f32[2,640,384]{2,1,0:T(8,128)S(1)} %first_rim.1.padded.old, f32[2,256,256]{2,1,0:T(8,128)S(1)} %copy-done, bf16[1,1,4,256,256]{4,3,2,1,0:T(8,128)(2,1)S(1)} %copy-done.1, ...), custom_call_target="tpu_custom_call" | custom-call | tf_op jit(solution)/shard_map/scan_terms/pallas_call | solution.py:142
  22.7 32.2 %merge.1 = (f32[2,640,384]{2,1,0:T(8,128)S(1)}, f32[2,256,256]{2,1,0:T(8,128)S(1)}) custom-call(f32[2,640,384]{2,1,0:T(8,128)S(1)} %get-tuple-element.8.grad, f32[2,256,256]{2,1,0:T(8,128)S(1)} %get-tuple-element.9.probe_grad, f32[2,640,384]{2,1,0:T(8,128)S(1)} %first_rim.1.padded.old, f32[2,256,256]{2,1,0:T(8,128)S(1)} %copy-done), custom_call_target="tpu_custom_call" | custom-call | tf_op jit(solution)/shard_map/merge/pallas_call | solution.py:460
  54.8 5.0 %scan_terms.3 = (f32[2,640,384]{2,1,0:T(8,128)S(1)}, f32[2,256,256]{2,1,0:T(8,128)S(1)}) custom-call(s32[4,2]{1,0:T(4,128)S(1)} %copy.11.starts, s32[1,1]{1,0:T(1,128)S(6)} %copy.14.counts, f32[2,640,384]{2,1,0:T(8,128)S(1)} %get-tuple-element.10.padded.old, f32[2,256,256]{2,1,0:T(8,128)S(1)} %get-tuple-element.11.probe, ...), custom_call_target="tpu_custom_call" | custom-call | tf_op jit(solution)/shard_map/scan_terms/pallas_call | solution.py:142
  59.8 26.2 %merge_last.1 = (f32[2,384,384]{2,1,0:T(8,128)S(1)}, f32[2,256,256]{2,1,0:T(8,128)S(1)}) custom-call(f32[2,640,384]{2,1,0:T(8,128)S(1)} %get-tuple-element.12.grad, f32[2,256,256]{2,1,0:T(8,128)S(1)} %get-tuple-element.13.probe_grad, f32[2,640,384]{2,1,0:T(8,128)S(1)} %get-tuple-element.10.padded.old, f32[2,256,256]{2,1,0:T(8,128)S(1)} %get-tuple-element.11.probe), custom_call_target="tpu_custom_call" | custom-call | tf_op jit(solution)/shard_map/merge_last/pallas_call | solution.py:460
  86.1 1.0 %copy.15 = f32[2,384,384]{2,1,0:T(8,128)} copy(f32[2,384,384]{2,1,0:T(8,128)S(1)} %get-tuple-element.16) | data formatting | bytes 2359296
  87.1 0.8 copy.16
Async XLA Ops:
  0.6 17.0 %copy-start.2 = (bf16[512,512]{1,0:T(8,128)(2,1)S(1)}, bf16[512,512]{1,0:T(8,128)(2,1)}, u32[]{:S(2)}) copy-start(bf16[512,512]{1,0:T(8,128)(2,1)} %constant.5.clone.table_b) | copy-start | bytes 1572868
  0.6 17.0 %copy-start.3 = (bf16[512,512]{1,0:T(8,128)(2,1)S(1)}, bf16[512,512]{1,0:T(8,128)(2,1)}, u32[]{:S(2)}) copy-start(bf16[512,512]{1,0:T(8,128)(2,1)} %constant.4.clone.table_a) | copy-start | bytes 1572868
  0.7 17.0 %copy-start.1 = (bf16[1,1,4,256,256]{4,3,2,1,0:T(8,128)(2,1)S(1)}, bf16[1,1,4,256,256]{4,3,2,1,0:T(8,128)(2,1)}, u32[]{:S(2)}) copy-start(bf16[1,1,4,256,256]{4,3,2,1,0:T(8,128)(2,1)} %amps.3) | copy-start | bytes 1572868
  0.7 17.0 %copy-start = (f32[2,256,256]{2,1,0:T(8,128)S(1)}, f32[2,256,256]{2,1,0:T(8,128)}, u32[]{:S(2)}) copy-start(f32[2,256,256]{2,1,0:T(8,128)} %probe.3) | copy-start | bytes 1572868
  2.3 1.3 %copy-start.4 = (f32[2,384,384]{2,1,0:T(8,128)S(1)}, f32[2,384,384]{2,1,0:T(8,128)}, u32[]{:S(2)}) copy-start(f32[2,384,384]{2,1,0:T(8,128)} %own.1) | copy-start | bytes 3538948

commit v4 on v3

--- a/solution.py
+++ b/solution.py
@@ -351,22 +351,6 @@
 
     late_sent = to_chips(late)
 
-    own_rows = pl.ds(chip * head + owned(tile) * fine, fine)
-    for made in spread:
-        on(owns(tile), made.wait_recv)
-
-    def close():
-        whole = probe_total[own_rows, :]
-        for k in range(1, n_tile):
-            whole = whole + probe_parts[(tile + k) % n_tile]
-        probe_out[core, own_rows, :] = probe[core, own_rows, :] + whole * scale
-
-    on(owns(tile), close)
-    place = probe_out.at[core, own_rows]
-    probe_back = [
-        links.copy(place, place, {"tile": (tile + k) % n_tile}, owns(tile))
-        for k in range(1, n_tile)
-    ]
     landed = []
 
     def update(span, sent):
@@ -383,19 +367,42 @@
         here = out.at[core, span]
         landed.append((links.copy(here, here, partner), None))
 
+    rims_back = []
+
+    def update_head(first, after):
+        for p in range(first, after):
+            update(spans[p], head_sent[p])
+            if not last:
+                rims_back.append(
+                    links.copy(out.at[core, spans[p]], out.at[core, rims[p]], up, above)
+                )
+
     update(early, early_sent)
-
+    update_head(0, parts // 2)
+
+    own_rows = pl.ds(chip * head + owned(tile) * fine, fine)
+    for made in spread:
+        on(owns(tile), made.wait_recv)
+
+    def close():
+        whole = probe_total[own_rows, :]
+        for k in range(1, n_tile):
+            whole = whole + probe_parts[(tile + k) % n_tile]
+        probe_out[core, own_rows, :] = probe[core, own_rows, :] + whole * scale
+
+    on(owns(tile), close)
+    place = probe_out.at[core, own_rows]
+    probe_back = [
+        links.copy(place, place, {"tile": (tile + k) % n_tile}, owns(tile))
+        for k in range(1, n_tile)
+    ]
+
+    update_head(parts // 2, parts)
     for k, made in zip(range(1, n_tile), probe_back):
         on(owns((tile + n_tile - k) % n_tile), made.wait_recv)
     here = probe_out.at[core, pl.ds(chip * head, head)]
     probe_across = [links.copy(here, here, links.on_chip(k)) for k in others]
     landed.append((links.copy(here, here, partner), None))
-
-    rims_back = []
-    for span, rim, sent in zip(spans, rims, head_sent):
-        update(span, sent)
-        if not last:
-            rims_back.append(links.copy(out.at[core, span], out.at[core, rim], up, above))
     update(late, late_sent)
     for k in others:
         probe_across[k - 1].wait_recv()

time: 88.1 us -> 85.8 us (0.974)
  Pallas kernels: 82.5 us -> 80.1 us
    pallas_call x2, Pallas kernels: 58.4 us -> 56.1 us  [merge(): pl.pallas_call(functools.partial(merge_kernel, n_tile, n_scan, parts, sca...]
where the time goes in v4:
time: 85.8 us; the launch traced here: 85.6 us
  Pallas kernels  80.1 us (93%)
  local copies, waits for them, and re-layouts  3.2 us (4%)
  between operations  1.53 us (2%)
    pallas_call x2, Pallas kernels, merge(): pl.pallas_call(functools.partial(merge_kernel, n_tile, n_scan, parts, sca...  56.1 us
    pallas_call x1, Pallas kernels, first_rim(): pl.pallas_call(functools.partial(rim_kernel, n_tile, n_scan, wave, parts)...  14.1 us
    pallas_call x2, Pallas kernels, scan_terms(): pl.pallas_call(scan_kernel, out_shape=(jax.ShapeDtypeStruct(padded.shape,...  9.98 us
    unnamed x12, local copies, waits for them, and re-layouts  3.1 us

profile of v4, /device:TPU:0, one launch (start us, length us, event | category | flops | bytes accessed | tf_op | source)
XLA Modules:
  0.0 85.6 jit_solution(7218885612217020732)
XLA Ops:
  0.6 0.0 copy-start.2
  0.6 0.0 copy-start.3
  0.7 0.0 copy-start.1
  0.7 0.0 copy-start
  1.5 0.7 add_bitcast_fusion
  2.2 0.1 copy.11.starts
  2.3 0.0 copy-start.4
  2.3 1.3 %copy-done.4 = f32[2,384,384]{2,1,0:T(8,128)S(1)} copy-done((f32[2,384,384]{2,1,0:T(8,128)S(1)}, f32[2,384,384]{2,1,0:T(8,128)}, u32[]{:S(2)}) %copy-start.4) | copy-done | bytes 1179672
  3.5 14.1 %first_rim.1.padded.old = f32[2,640,384]{2,1,0:T(8,128)S(1)} custom-call(f32[2,384,384]{2,1,0:T(8,128)S(1)} %copy-done.4), custom_call_target="tpu_custom_call" | custom-call | tf_op jit(solution)/shard_map/first_rim/pallas_call | solution.py:439
  17.7 0.0 copy-done.2
  17.7 0.0 copy-done.3
  17.7 0.0 copy-done.1
  17.7 0.0 copy-done
  17.7 5.0 %scan_terms.2 = (f32[2,640,384]{2,1,0:T(8,128)S(1)}, f32[2,256,256]{2,1,0:T(8,128)S(1)}) custom-call(s32[4,2]{1,0:T(4,128)S(1)} %copy.11.starts, s32[1,1]{1,0:T(1,128)S(6)} %copy.14.counts, f32[2,640,384]{2,1,0:T(8,128)S(1)} %first_rim.1.padded.old, f32[2,256,256]{2,1,0:T(8,128)S(1)} %copy-done, bf16[1,1,4,256,256]{4,3,2,1,0:T(8,128)(2,1)S(1)} %copy-done.1, ...), custom_call_target="tpu_custom_call" | custom-call | tf_op jit(solution)/shard_map/scan_terms/pallas_call | solution.py:142
  22.7 29.8 %merge.1 = (f32[2,640,384]{2,1,0:T(8,128)S(1)}, f32[2,256,256]{2,1,0:T(8,128)S(1)}) custom-call(f32[2,640,384]{2,1,0:T(8,128)S(1)} %get-tuple-element.8.grad, f32[2,256,256]{2,1,0:T(8,128)S(1)} %get-tuple-element.9.probe_grad, f32[2,640,384]{2,1,0:T(8,128)S(1)} %first_rim.1.padded.old, f32[2,256,256]{2,1,0:T(8,128)S(1)} %copy-done), custom_call_target="tpu_custom_call" | custom-call | tf_op jit(solution)/shard_map/merge/pallas_call | solution.py:467
  52.5 5.0 %scan_terms.3 = (f32[2,640,384]{2,1,0:T(8,128)S(1)}, f32[2,256,256]{2,1,0:T(8,128)S(1)}) custom-call(s32[4,2]{1,0:T(4,128)S(1)} %copy.11.starts, s32[1,1]{1,0:T(1,128)S(6)} %copy.14.counts, f32[2,640,384]{2,1,0:T(8,128)S(1)} %get-tuple-element.10.padded.old, f32[2,256,256]{2,1,0:T(8,128)S(1)} %get-tuple-element.11.probe, ...), custom_call_target="tpu_custom_call" | custom-call | tf_op jit(solution)/shard_map/scan_terms/pallas_call | solution.py:142
  57.4 26.3 %merge_last.1 = (f32[2,384,384]{2,1,0:T(8,128)S(1)}, f32[2,256,256]{2,1,0:T(8,128)S(1)}) custom-call(f32[2,640,384]{2,1,0:T(8,128)S(1)} %get-tuple-element.12.grad, f32[2,256,256]{2,1,0:T(8,128)S(1)} %get-tuple-element.13.probe_grad, f32[2,640,384]{2,1,0:T(8,128)S(1)} %get-tuple-element.10.padded.old, f32[2,256,256]{2,1,0:T(8,128)S(1)} %get-tuple-element.11.probe), custom_call_target="tpu_custom_call" | custom-call | tf_op jit(solution)/shard_map/merge_last/pallas_call | solution.py:467
  83.8 1.0 %copy.15 = f32[2,384,384]{2,1,0:T(8,128)} copy(f32[2,384,384]{2,1,0:T(8,128)S(1)} %get-tuple-element.16) | data formatting | bytes 2359296
  84.8 0.8 copy.16
Async XLA Ops:
  0.6 17.0 %copy-start.2 = (bf16[512,512]{1,0:T(8,128)(2,1)S(1)}, bf16[512,512]{1,0:T(8,128)(2,1)}, u32[]{:S(2)}) copy-start(bf16[512,512]{1,0:T(8,128)(2,1)} %constant.5.clone.table_b) | copy-start | bytes 1572868
  0.6 17.0 %copy-start.3 = (bf16[512,512]{1,0:T(8,128)(2,1)S(1)}, bf16[512,512]{1,0:T(8,128)(2,1)}, u32[]{:S(2)}) copy-start(bf16[512,512]{1,0:T(8,128)(2,1)} %constant.4.clone.table_a) | copy-start | bytes 1572868
  0.7 17.0 %copy-start.1 = (bf16[1,1,4,256,256]{4,3,2,1,0:T(8,128)(2,1)S(1)}, bf16[1,1,4,256,256]{4,3,2,1,0:T(8,128)(2,1)}, u32[]{:S(2)}) copy-start(bf16[1,1,4,256,256]{4,3,2,1,0:T(8,128)(2,1)} %amps.3) | copy-start | bytes 1572868
  0.7 17.0 %copy-start = (f32[2,256,256]{2,1,0:T(8,128)S(1)}, f32[2,256,256]{2,1,0:T(8,128)}, u32[]{:S(2)}) copy-start(f32[2,256,256]{2,1,0:T(8,128)} %probe.3) | copy-start | bytes 1572868
  2.3 1.3 %copy-start.4 = (f32[2,384,384]{2,1,0:T(8,128)S(1)}, f32[2,384,384]{2,1,0:T(8,128)}, u32[]{:S(2)}) copy-start(f32[2,384,384]{2,1,0:T(8,128)} %own.1) | copy-start | bytes 3538948

commit v5 on v4

--- a/solution.py
+++ b/solution.py
@@ -302,54 +302,35 @@
         piece = probe_total.at[pl.ds(links.chip_at(k) * head, head)]
         probe_sent.append(links.copy(piece, probe_in.at[chip], links.on_chip(k)))
 
-    rims_sent = []
-    for got, span, landing in zip(got_rims, rims, spans):
-        got.wait_recv()
-        total[span, :] = grad[core, span, :] + core_in[span, :]
-        rims_sent.append(links.copy(total.at[span], rim_back.at[landing], down, below))
+    def owns(index):
+        return None if owners == n_tile else index < owners
+
+    def owned(index):
+        return index if owners == n_tile else jnp.minimum(index, owners - 1)
 
     def to_chips(span):
         return [
             links.copy(total.at[span], chip_in.at[chip, span], links.on_chip(k)) for k in others
         ]
 
-    tail_rows = pl.ds(wave, rest)
-    got_tail.wait_recv()
-    total[tail_rows, :] = grad[core, tail_rows, :] + core_in[tail_rows, :]
-    early, late = pl.ds(wave, rest // 2), pl.ds(wave + rest // 2, rest // 2)
-    early_sent = to_chips(early)
-
-    inverse = RATE / (
-        jnp.max(probe[0] * probe[0] + probe[1] * probe[1], axis=(0, 1), keepdims=True) + 1e-06
-    )
-    got_head.wait_recv()
-
-    def owns(index):
-        return None if owners == n_tile else index < owners
-
-    def owned(index):
-        return index if owners == n_tile else jnp.minimum(index, owners - 1)
-
-    head_sent, spread = [], []
-    for p, (span, made) in enumerate(zip(spans, rims_sent)):
-        on(above, made.wait_recv)
-        back = jnp.where(above, rim_back[span, :], 0.0)
-        total[span, :] = grad[core, span, :] + core_in[span, :] + back
-        head_sent.append(to_chips(span))
-        if p == 0:
-            for made in probe_sent:
-                made.wait_recv()
-            mine = pl.ds(chip * head, head)
-            whole = probe_total[mine, :]
-            for k in others:
-                whole = whole + probe_in[links.chip_at(k)]
-            probe_total[mine, :] = whole
-            for k in range(1, n_tile):
-                to = (tile + k) % n_tile
-                piece = probe_total.at[pl.ds(chip * head + owned(to) * fine, fine)]
-                spread.append(links.copy(piece, probe_parts.at[tile], {"tile": to}, owns(to)))
-
-    late_sent = to_chips(late)
+    rims_sent = []
+
+    def send_rims(first, after):
+        for p in range(first, after):
+            span = rims[p]
+            got_rims[p].wait_recv()
+            total[span, :] = grad[core, span, :] + core_in[span, :]
+            rims_sent.append(links.copy(total.at[span], rim_back.at[spans[p]], down, below))
+
+    head_sent = []
+
+    def send_head(first, after):
+        for p in range(first, after):
+            span = spans[p]
+            on(above, rims_sent[p].wait_recv)
+            back = jnp.where(above, rim_back[span, :], 0.0)
+            total[span, :] = grad[core, span, :] + core_in[span, :] + back
+            head_sent.append(to_chips(span))
 
     landed = []
 
@@ -377,8 +358,38 @@
                     links.copy(out.at[core, spans[p]], out.at[core, rims[p]], up, above)
                 )
 
+    half = parts // 2
+    send_rims(0, half)
+
+    tail_rows = pl.ds(wave, rest)
+    got_tail.wait_recv()
+    total[tail_rows, :] = grad[core, tail_rows, :] + core_in[tail_rows, :]
+    early, late = pl.ds(wave, rest // 2), pl.ds(wave + rest // 2, rest // 2)
+    early_sent = to_chips(early)
+
+    for made in probe_sent:
+        made.wait_recv()
+    mine = pl.ds(chip * head, head)
+    whole = probe_total[mine, :]
+    for k in others:
+        whole = whole + probe_in[links.chip_at(k)]
+    probe_total[mine, :] = whole
+    spread = []
+    for k in range(1, n_tile):
+        to = (tile + k) % n_tile
+        piece = probe_total.at[pl.ds(chip * head + owned(to) * fine, fine)]
+        spread.append(links.copy(piece, probe_parts.at[tile], {"tile": to}, owns(to)))
+
+    send_rims(half, parts)
+
+    inverse = RATE / (
+        jnp.max(probe[0] * probe[0] + probe[1] * probe[1], axis=(0, 1), keepdims=True) + 1e-06
+    )
+    got_head.wait_recv()
+
+    send_head(0, half)
+    late_sent = to_chips(late)
     update(early, early_sent)
-    update_head(0, parts // 2)
 
     own_rows = pl.ds(chip * head + owned(tile) * fine, fine)
     for made in spread:
@@ -397,13 +408,16 @@
         for k in range(1, n_tile)
     ]
 
-    update_head(parts // 2, parts)
+    for p in range(half, parts):
+        update_head(p - half, p - half + 1)
+        send_head(p, p + 1)
+    update(late, late_sent)
+    update_head(half, parts)
     for k, made in zip(range(1, n_tile), probe_back):
         on(owns((tile + n_tile - k) % n_tile), made.wait_recv)
     here = probe_out.at[core, pl.ds(chip * head, head)]
     probe_across = [links.copy(here, here, links.on_chip(k)) for k in others]
     landed.append((links.copy(here, here, partner), None))
-    update(late, late_sent)
     for k in others:
         probe_across[k - 1].wait_recv()
         here = probe_out.at[core, pl.ds(links.chip_at(chips - k) * head, head)]

time: 85.8 us -> 85.4 us (level)
  no operation moved by 1% of the time
where the time goes in v5:
time: 85.4 us; the launch traced here: 85.5 us
  Pallas kernels  80.1 us (94%)
  local copies, waits for them, and re-layouts  3.2 us (4%)
  between operations  1.53 us (2%)
    pallas_call x2, Pallas kernels, merge(): pl.pallas_call(functools.partial(merge_kernel, n_tile, n_scan, parts, sca...  56.1 us
    pallas_call x1, Pallas kernels, first_rim(): pl.pallas_call(functools.partial(rim_kernel, n_tile, n_scan, wave, parts)...  14.1 us
    pallas_call x2, Pallas kernels, scan_terms(): pl.pallas_call(scan_kernel, out_shape=(jax.ShapeDtypeStruct(padded.shape,...  9.9 us
    unnamed x12, local copies, waits for them, and re-layouts  3.1 us

profile of v5, /device:TPU:0, one launch (start us, length us, event | category | flops | bytes accessed | tf_op | source)
XLA Modules:
  0.0 85.5 jit_solution(5558542669054609706)
XLA Ops:
  0.6 0.0 copy-start.2
  0.6 0.0 copy-start.3
  0.7 0.0 copy-start.1
  0.7 0.0 copy-start
  1.5 0.7 add_bitcast_fusion
  2.2 0.1 copy.11.starts
  2.3 0.0 copy-start.4
  2.3 1.3 %copy-done.4 = f32[2,384,384]{2,1,0:T(8,128)S(1)} copy-done((f32[2,384,384]{2,1,0:T(8,128)S(1)}, f32[2,384,384]{2,1,0:T(8,128)}, u32[]{:S(2)}) %copy-start.4) | copy-done | bytes 1179672
  3.5 14.1 %first_rim.1.padded.old = f32[2,640,384]{2,1,0:T(8,128)S(1)} custom-call(f32[2,384,384]{2,1,0:T(8,128)S(1)} %copy-done.4), custom_call_target="tpu_custom_call" | custom-call | tf_op jit(solution)/shard_map/first_rim/pallas_call | solution.py:453
  17.7 0.0 copy-done.2
  17.7 0.0 copy-done.3
  17.7 0.0 copy-done.1
  17.7 0.0 copy-done
  17.7 5.0 %scan_terms.2 = (f32[2,640,384]{2,1,0:T(8,128)S(1)}, f32[2,256,256]{2,1,0:T(8,128)S(1)}) custom-call(s32[4,2]{1,0:T(4,128)S(1)} %copy.11.starts, s32[1,1]{1,0:T(1,128)S(6)} %copy.14.counts, f32[2,640,384]{2,1,0:T(8,128)S(1)} %first_rim.1.padded.old, f32[2,256,256]{2,1,0:T(8,128)S(1)} %copy-done, bf16[1,1,4,256,256]{4,3,2,1,0:T(8,128)(2,1)S(1)} %copy-done.1, ...), custom_call_target="tpu_custom_call" | custom-call | tf_op jit(solution)/shard_map/scan_terms/pallas_call | solution.py:142
  22.7 27.5 %merge.1 = (f32[2,640,384]{2,1,0:T(8,128)S(1)}, f32[2,256,256]{2,1,0:T(8,128)S(1)}) custom-call(f32[2,640,384]{2,1,0:T(8,128)S(1)} %get-tuple-element.8.grad, f32[2,256,256]{2,1,0:T(8,128)S(1)} %get-tuple-element.9.probe_grad, f32[2,640,384]{2,1,0:T(8,128)S(1)} %first_rim.1.padded.old, f32[2,256,256]{2,1,0:T(8,128)S(1)} %copy-done), custom_call_target="tpu_custom_call" | custom-call | tf_op jit(solution)/shard_map/merge/pallas_call | solution.py:481
  50.1 5.0 %scan_terms.3 = (f32[2,640,384]{2,1,0:T(8,128)S(1)}, f32[2,256,256]{2,1,0:T(8,128)S(1)}) custom-call(s32[4,2]{1,0:T(4,128)S(1)} %copy.11.starts, s32[1,1]{1,0:T(1,128)S(6)} %copy.14.counts, f32[2,640,384]{2,1,0:T(8,128)S(1)} %get-tuple-element.10.padded.old, f32[2,256,256]{2,1,0:T(8,128)S(1)} %get-tuple-element.11.probe, ...), custom_call_target="tpu_custom_call" | custom-call | tf_op jit(solution)/shard_map/scan_terms/pallas_call | solution.py:142
  55.1 28.6 %merge_last.1 = (f32[2,384,384]{2,1,0:T(8,128)S(1)}, f32[2,256,256]{2,1,0:T(8,128)S(1)}) custom-call(f32[2,640,384]{2,1,0:T(8,128)S(1)} %get-tuple-element.12.grad, f32[2,256,256]{2,1,0:T(8,128)S(1)} %get-tuple-element.13.probe_grad, f32[2,640,384]{2,1,0:T(8,128)S(1)} %get-tuple-element.10.padded.old, f32[2,256,256]{2,1,0:T(8,128)S(1)} %get-tuple-element.11.probe), custom_call_target="tpu_custom_call" | custom-call | tf_op jit(solution)/shard_map/merge_last/pallas_call | solution.py:481
  83.7 1.0 %copy.15 = f32[2,384,384]{2,1,0:T(8,128)} copy(f32[2,384,384]{2,1,0:T(8,128)S(1)} %get-tuple-element.16) | data formatting | bytes 2359296
  84.7 0.8 copy.16
Async XLA Ops:
  0.6 17.0 %copy-start.2 = (bf16[512,512]{1,0:T(8,128)(2,1)S(1)}, bf16[512,512]{1,0:T(8,128)(2,1)}, u32[]{:S(2)}) copy-start(bf16[512,512]{1,0:T(8,128)(2,1)} %constant.5.clone.table_b) | copy-start | bytes 1572868
  0.6 17.0 %copy-start.3 = (bf16[512,512]{1,0:T(8,128)(2,1)S(1)}, bf16[512,512]{1,0:T(8,128)(2,1)}, u32[]{:S(2)}) copy-start(bf16[512,512]{1,0:T(8,128)(2,1)} %constant.4.clone.table_a) | copy-start | bytes 1572868
  0.7 17.0 %copy-start.1 = (bf16[1,1,4,256,256]{4,3,2,1,0:T(8,128)(2,1)S(1)}, bf16[1,1,4,256,256]{4,3,2,1,0:T(8,128)(2,1)}, u32[]{:S(2)}) copy-start(bf16[1,1,4,256,256]{4,3,2,1,0:T(8,128)(2,1)} %amps.3) | copy-start | bytes 1572868
  0.7 17.0 %copy-start = (f32[2,256,256]{2,1,0:T(8,128)S(1)}, f32[2,256,256]{2,1,0:T(8,128)}, u32[]{:S(2)}) copy-start(f32[2,256,256]{2,1,0:T(8,128)} %probe.3) | copy-start | bytes 1572868
  2.3 1.3 %copy-start.4 = (f32[2,384,384]{2,1,0:T(8,128)S(1)}, f32[2,384,384]{2,1,0:T(8,128)}, u32[]{:S(2)}) copy-start(f32[2,384,384]{2,1,0:T(8,128)} %own.1) | copy-start | bytes 3538948
